TPU v7x, 512 devices: a whole 4x8x8 slice. The times are simulated.
512 devices in a mesh: lev: 2 (over core), lat: 8 (over z_lo, x), lon: 32 (over z_hi, y).
Axes of the slice: x: 4, y: 8, z: 8 (z_hi: 4, z_lo: 2; z = z_hi * 2 + z_lo), core: 2. Of those that a mesh axis runs over, the one named last changes fastest.
Arguments:
- tokens: bfloat16 [4, 48, 768, 384], P('lev', 'lat', 'lon'), may hold values from -6 to 6
- cotangent: bfloat16 [4, 48, 768, 384], P('lev', 'lat', 'lon'), may hold values from -6 to 6
- w_qkv: bfloat16 [384, 1152], replicated, may hold values from -16 to 16, as said below
- w_proj: bfloat16 [384, 384], replicated, may hold values from -0.609375 to 0.609375
- bias_table: float32 [8, 12, 3312], P('lat'), may hold values from -5 to 5
- bias_index: int32 [8, 144, 144], P('lat'), may hold values from 0 to 3311
- region_ids: int32 [48, 768], P('lat', 'lon'), may hold values from 0 to 2
Outputs:
- block_out: bfloat16 [4, 48, 768, 384], P('lev', 'lat', 'lon')
- grad_tokens: bfloat16 [4, 48, 768, 384], P('lev', 'lat', 'lon')
- grad_qkv: float32 [384, 1152], P('lat', ('lev', 'lon'))
- grad_proj: float32 [384, 384], P('lat', ('lev', 'lon'))
- grad_table: float32 [8, 12, 3312], P('lat')
Inputs may be any that keep to these rules, and one draw needn't show every extreme that they name: `w_qkv`: columns 0 to 383 project queries, 384 to 767 keys, the rest values.
All inputs are finite; a program needn't handle non-finite values.
Results may differ from a plain program's by a relative error of at most 0.012.
The roundings to bfloat16 on the way count: a program that leaves them out, or rounds other values in their place, can miss the bound.
Values may be sent and summed in bfloat16 or wider, within the bound.
A program may use at most 64 MiB of HBM per device.

v0:
```python
import math

import jax
import jax.numpy as jnp
from jax import lax
from jax.sharding import PartitionSpec as P

WLEV = 2
WLAT = 6
WLON = 12
WIN = 144


def shifted(block, axis, distance):
    devices = range(lax.axis_size(axis))
    route = [((i - distance) % len(devices), i) for i in devices]
    return lax.ppermute(block, axis, route)


def rim_lat(piece, offset):
    return shifted(piece, "lat", offset)


def rim_lon(piece, offset):
    return shifted(piece, "lon", offset)


def lat_in(field):
    half_rows = WLAT // 2
    return jnp.concatenate([field[:, half_rows:], rim_lat(field[:, :half_rows], -1)], 1)


def lon_in(field):
    half_cols = WLON // 2
    return jnp.concatenate([field[:, :, half_cols:], rim_lon(field[:, :, :half_cols], -1)], 2)


def lat_out(field):
    half_rows = WLAT // 2
    return jnp.concatenate([rim_lat(field[:, -half_rows:], 1), field[:, :-half_rows]], 1)


def lon_out(field):
    half_cols = WLON // 2
    return jnp.concatenate([rim_lon(field[:, :, -half_cols:], 1), field[:, :, :-half_cols]], 2)


def roll_in(field):
    return lon_in(lat_in(field))


def roll_out(field):
    return lon_out(lat_out(field))


def to_windows(field):
    levels, rows, columns, width = field.shape
    shaped = field.reshape(levels // WLEV, WLEV, rows // WLAT, WLAT, columns // WLON, WLON, width)
    shaped = shaped.transpose(2, 0, 4, 1, 3, 5, 6)
    return shaped.reshape(rows // WLAT, levels // WLEV * (columns // WLON), WIN, width)


def from_windows(blocks, levels, columns):
    types_here, count, win_size, width = blocks.shape
    shaped = blocks.reshape(types_here, levels // WLEV, columns // WLON, WLEV, WLAT, WLON, width)
    shaped = shaped.transpose(1, 3, 0, 4, 2, 5, 6)
    return shaped.reshape(levels, types_here * WLAT, columns, width)


def region_windows(region, level_windows):
    rows, columns = region.shape
    shaped = region.reshape(rows // WLAT, WLAT, columns // WLON, WLON).transpose(0, 2, 1, 3)
    shaped = shaped.reshape(rows // WLAT, columns // WLON, WLAT * WLON)
    shaped = jnp.tile(shaped, (1, 1, WLEV))
    shaped = shaped[:, None]
    return shaped.reshape(rows // WLAT, level_windows * (columns // WLON), WIN)


def window_pass(windows, cot_windows, index_table, bias_rows, region_rows, w_qkv, w_proj):
    count, win_size, width = windows.shape
    heads = bias_rows.shape[0]
    head_size = width // heads
    factor = head_size ** (-0.5)
    flat = windows.reshape(count * win_size, width).astype(jnp.float32)
    center = flat - jnp.mean(flat, axis=-1, keepdims=True)
    inverse = lax.rsqrt(jnp.mean(center * center, axis=-1, keepdims=True) + 1e-05)
    unit_rows = center * inverse
    normed = unit_rows.astype(jnp.bfloat16)
    packed = jnp.dot(normed, w_qkv, preferred_element_type=jnp.float32).astype(jnp.bfloat16)
    packed = packed.reshape(count, win_size, 3, heads, head_size)
    query_rows = packed[:, :, 0]
    key_rows = packed[:, :, 1]
    value_rows = packed[:, :, 2]
    scores = (
        jnp.einsum("bihd,bjhd->bhij", query_rows, key_rows, preferred_element_type=jnp.float32)
        * factor
    )
    scores = scores + jnp.take(bias_rows, index_table, axis=1)[None]
    allowed = (region_rows[:, :, None] == region_rows[:, None, :])[:, None]
    scores = jnp.where(allowed, scores, -1e30)
    top = jnp.max(scores, axis=-1, keepdims=True)
    expo = jnp.exp(scores - top)
    probs = expo / jnp.sum(expo, axis=-1, keepdims=True)
    probs_b = probs.astype(jnp.bfloat16)
    mixed = jnp.einsum("bhij,bjhd->bihd", probs_b, value_rows, preferred_element_type=jnp.float32)
    mixed = mixed.astype(jnp.bfloat16).reshape(count * win_size, width)
    branch = jnp.dot(mixed, w_proj, preferred_element_type=jnp.float32).astype(jnp.bfloat16)
    cot_flat = cot_windows.reshape(count * win_size, width)
    grad_proj = jnp.einsum("tc,td->cd", mixed, cot_flat, preferred_element_type=jnp.float32)
    grad_mixed = jnp.einsum("td,cd->tc", cot_flat, w_proj, preferred_element_type=jnp.float32)
    grad_mixed = grad_mixed.astype(jnp.bfloat16).reshape(count, win_size, heads, head_size)
    grad_probs = jnp.einsum(
        "bihd,bjhd->bhij", grad_mixed, value_rows, preferred_element_type=jnp.float32
    )
    grad_value = jnp.einsum(
        "bhij,bihd->bjhd", probs_b, grad_mixed, preferred_element_type=jnp.float32
    )
    grad_value = grad_value.astype(jnp.bfloat16)
    grad_scores = probs * (grad_probs - jnp.sum(probs * grad_probs, axis=-1, keepdims=True))
    summed = jnp.sum(grad_scores, axis=0).reshape(heads, win_size * win_size)
    grad_bias = jax.ops.segment_sum(
        summed.T, index_table.reshape(-1), num_segments=bias_rows.shape[1]
    ).T
    scaled = (grad_scores * factor).astype(jnp.bfloat16)
    grad_query = jnp.einsum("bhij,bjhd->bihd", scaled, key_rows, preferred_element_type=jnp.float32)
    grad_key = jnp.einsum("bhij,bihd->bjhd", scaled, query_rows, preferred_element_type=jnp.float32)
    grad_packed = jnp.stack(
        [grad_query.astype(jnp.bfloat16), grad_key.astype(jnp.bfloat16), grad_value], 2
    )
    grad_packed = grad_packed.reshape(count * win_size, 3 * width)
    grad_qkv = jnp.einsum("tc,te->ce", normed, grad_packed, preferred_element_type=jnp.float32)
    grad_normed = jnp.einsum("te,ce->tc", grad_packed, w_qkv, preferred_element_type=jnp.float32)
    grad_rows = inverse * (
        grad_normed
        - jnp.mean(grad_normed, axis=-1, keepdims=True)
        - unit_rows * jnp.mean(grad_normed * unit_rows, axis=-1, keepdims=True)
    )
    grad_rows = grad_rows.astype(jnp.bfloat16).reshape(count, win_size, width)
    return (branch.reshape(count, win_size, width), grad_rows, grad_qkv, grad_proj, grad_bias)


def body(tokens, cotangent, w_qkv, w_proj, bias_table, bias_index, region_ids):
    levels, rows, columns, width = tokens.shape
    windows = to_windows(roll_in(tokens))
    cot_windows = to_windows(roll_in(cotangent))
    regions = region_windows(region_ids, levels // WLEV)
    branch, grad_rows, part_qkv, part_proj, grad_bias = window_pass(
        windows[0], cot_windows[0], bias_index[0], bias_table[0], regions[0], w_qkv, w_proj
    )
    branches = [branch]
    grad_blocks = [grad_rows]
    table_parts = [grad_bias]
    branch_field = from_windows(jnp.stack(branches, 0), levels, columns)
    grad_field = from_windows(jnp.stack(grad_blocks, 0), levels, columns)
    block_out = (tokens.astype(jnp.float32) + roll_out(branch_field).astype(jnp.float32)).astype(
        jnp.bfloat16
    )
    grad_tokens = (cotangent.astype(jnp.float32) + roll_out(grad_field).astype(jnp.float32)).astype(
        jnp.bfloat16
    )
    token_count = (
        levels * lax.axis_size("lev") * rows * lax.axis_size("lat") * columns * lax.axis_size("lon")
    )
    norm_factor = 1.0 / math.sqrt(token_count)
    wide_qkv, wide_proj = (
        lax.psum_scatter(part_qkv, ("lev", "lon"), scatter_dimension=1, tiled=True),
        lax.psum_scatter(part_proj, ("lev", "lon"), scatter_dimension=1, tiled=True),
    )
    grad_qkv, grad_proj = (
        lax.psum_scatter(wide_qkv, "lat", scatter_dimension=0, tiled=True),
        lax.psum_scatter(wide_proj, "lat", scatter_dimension=0, tiled=True),
    )
    grad_table = lax.psum(jnp.stack(table_parts, 0), ("lev", "lon"))
    return (block_out, grad_tokens, grad_qkv * norm_factor, grad_proj * norm_factor, grad_table)


def solution(mesh):
    return jax.shard_map(
        body,
        mesh=mesh,
        in_specs=(
            P("lev", "lat", "lon", None),
            P("lev", "lat", "lon", None),
            P(),
            P(),
            P("lat", None, None),
            P("lat", None, None),
            P("lat", "lon"),
        ),
        out_specs=(
            P("lev", "lat", "lon", None),
            P("lev", "lat", "lon", None),
            P("lat", ("lev", "lon")),
            P("lat", ("lev", "lon")),
            P("lat", None, None),
        ),
        check_vma=False,
    )
```

profile of v0, /device:TPU:6, one launch (start us, length us, event | category | flops | bytes accessed | tf_op | source)
XLA Modules:
  0.0 990.0 jit_solution(16890992788400325430)
XLA Ops:
  8.9 2.7 collective-permute-start
  12.6 2.4 collective-permute-start.4
  18.6 38.7 %gather_fusion = f32[20736,12]{1,0:T(8,128)} fusion(f32[12,3312]{0,1:T(8,128)S(1)} %bitcast.87, s32[21504]{0:T(1024)S(1)} %pad_clamp_fusion), kind=kCustom, calls=%fused_computation | custom fusion | bytes 2073600 | tf_op jit(solution)/shard_map/jit(_take)/gather | solution.py:98
  57.3 11.6 %copy.102 = f32[144,144,12]{0,1,2:T(8,128)S(1)} copy(f32[144,144,12]{2,1,0:T(8,128)} %bitcast.88) | data formatting | bytes 1990656 | tf_op jit(solution)/shard_map/jit(_take)/gather | solution.py:98
  72.3 13.8 %collective-permute-start.1 = (bf16[2,6,6,384]{3,2,1,0:T(8,128)(2,1)S(1)}, bf16[2,6,6,384]{3,2,1,0:T(8,128)(2,1)S(1)}, u32[]{:S(2)}, u32[]{:S(2)}) collective-permute-start(bf16[2,6,6,384]{3,2,1,0:T(8,128)(2,1)S(1)} %pad_maximum_fusion.5), channel_id=1, source_target_pairs={{1,0},{2,1},{3,2},{4,3},{5,4},{6,5},{7,6},{8,7},{9,8},{10,9},{11,1... | collective-permute-start | bytes 165896 | tf_op jit(solution)/shard_map/ppermute | solution.py:17
  86.8 3.2 collective-permute-start.5
  94.2 3.6 reshape.151
  108.4 4.4 fusion.50
  112.8 3.4 fusion.10
  117.2 2.5 fusion.20
  119.7 7.0 fusion.12
  126.7 6.2 fusion.11
  134.0 7.6 fusion.51
  151.8 6.9 copy.119
  160.6 113.8 %scatter_custom_fusion = f32[3312,12]{1,0:T(8,128)} fusion(s32[20736]{0:T(1024)} %reshape.173, f32[20736,12]{1,0:T(8,128)} %copy.119, f32[]{:T(128)} %constant.10.clone.1), kind=kCustom, calls=%fused_computation.31 | custom fusion | flops 248832 | bytes 159488 | tf_op jit(solution)/shard_map/scatter-add | solution.py:121
  277.8 5.6 collective-permute-start.2
  285.0 3.1 collective-permute-start.6
  288.2 2.6 collective-permute-start.3
  291.7 2.6 collective-permute-start.7
  294.3 5.1 collective-permute-done.3
  303.6 574.9 %all-reduce.5.cloned.1.call-done = (f32[384,1152]{0,1:T(8,128)}, f32[384,384]{0,1:T(8,128)}, f32[1,12,3312]{1,2,0:T(8,128)}) async-done(((f32[384,1152]{0,1:T(8,128)}, f32[384,384]{0,1:T(8,128)}, f32[1,12,3312]{1,2,0:T(8,128)}), (f32[384,1152]{0,1:T(8,128)}, f32[384,384]{0,1:T(8,128)}, f32[1,12,3312]{1,2,0:T(8,128)})) %all-reduce.5.cloned.1.call-update) | async-done | bytes 2518288
  881.8 2.6 copy.122
  884.4 53.5 %reduce-scatter.9.cloned.1.call-done = f32[48,6]{1,0:T(8,128)} async-done(((f32[384,6]{1,0:T(8,128)}), f32[48,6]{1,0:T(8,128)}) %reduce-scatter.9.cloned.1.call-update) | async-done | bytes 1168
  939.3 42.7 %reduce-scatter.7.cloned.1.call-done = f32[48,18]{1,0:T(8,128)} async-done(((f32[384,18]{1,0:T(8,128)}), f32[48,18]{1,0:T(8,128)}) %reduce-scatter.7.cloned.1.call-update) | async-done | bytes 3472
  (137 shorter events, 53.8 us)
Async XLA Ops:
  7.2 85.2 %copy-start = (bf16[384,1152]{1,0:T(8,128)(2,1)S(1)}, bf16[384,1152]{1,0:T(8,128)(2,1)}, u32[]{:S(2)}) copy-start(bf16[384,1152]{1,0:T(8,128)(2,1)} %param.9) | copy-start | bytes 2654212
  7.2 871.3 %all-reduce.5.cloned.1.call-start = ((), (), s32[]{:S(2)}) async-start(), calls=%async_computation.4 | async-start | bytes 8110080
  8.9 63.3 %collective-permute-start = (bf16[2,3,24,384]{3,2,1,0:T(8,128)(2,1)}, bf16[2,3,24,384]{3,2,1,0:T(8,128)(2,1)S(1)}, u32[]{:S(2)}, u32[]{:S(2)}) collective-permute-start(bf16[2,3,24,384]{3,2,1,0:T(8,128)(2,1)} %get-tuple-element.40), channel_id=1, source_target_pairs={{32,0},{64,32},{96,64},{128,96},{160,128},{192,160},{224,192},{0,2... | collective-permute-start | bytes 331784 | tf_op jit(solution)/shard_map/ppermute | solution.py:17
  12.6 73.5 %collective-permute-start.4 = (bf16[2,3,24,384]{3,2,1,0:T(8,128)(2,1)S(1)}, bf16[2,3,24,384]{3,2,1,0:T(8,128)(2,1)S(1)}, u32[]{:S(2)}, u32[]{:S(2)}) collective-permute-start(bf16[2,3,24,384]{3,2,1,0:T(8,128)(2,1)S(1)} %get-tuple-element.36), channel_id=1, source_target_pairs={{32,0},{64,32},{96,64},{128,96},{160,128},{192,160},{224,192},{0,2... | collective-permute-start | bytes 331784 | tf_op jit(solution)/shard_map/ppermute | solution.py:17
  57.3 11.7 %copy-start.20 = (s32[6,24]{1,0:T(8,128)S(1)}, s32[6,24]{1,0:T(8,128)}, u32[]{:S(2)}) copy-start(s32[6,24]{1,0:T(8,128)} %param.13) | copy-start | bytes 1732
  72.3 17.9 %collective-permute-start.1 = (bf16[2,6,6,384]{3,2,1,0:T(8,128)(2,1)S(1)}, bf16[2,6,6,384]{3,2,1,0:T(8,128)(2,1)S(1)}, u32[]{:S(2)}, u32[]{:S(2)}) collective-permute-start(bf16[2,6,6,384]{3,2,1,0:T(8,128)(2,1)S(1)} %pad_maximum_fusion.5), channel_id=1, source_target_pairs={{1,0},{2,1},{3,2},{4,3},{5,4},{6,5},{7,6},{8,7},{9,8},{10,9},{11,1... | collective-permute-start | bytes 165896 | tf_op jit(solution)/shard_map/ppermute | solution.py:17
  86.8 13.0 %collective-permute-start.5 = (bf16[2,6,6,384]{3,2,1,0:T(8,128)(2,1)}, bf16[2,6,6,384]{3,2,1,0:T(8,128)(2,1)}, u32[]{:S(2)}, u32[]{:S(2)}) collective-permute-start(bf16[2,6,6,384]{3,2,1,0:T(8,128)(2,1)} %pad_maximum_fusion.4), channel_id=1, source_target_pairs={{1,0},{2,1},{3,2},{4,3},{5,4},{6,5},{7,6},{8,7},{9,8},{10,9},{11,1... | collective-permute-start | bytes 165896 | tf_op jit(solution)/shard_map/ppermute | solution.py:17
  91.5 8.2 copy-start.1
  97.8 10.6 %copy-start.19 = (pred[2,144,144]{1,2,0:T(8,128)(4,1)S(1)}, pred[2,144,144]{1,2,0:T(8,128)(4,1)}, u32[]{:S(2)}) copy-start(pred[2,144,144]{1,2,0:T(8,128)(4,1)} %broadcast_compare_fusion) | copy-start | bytes 124420
  99.7 8.7 copy-start.5
  119.7 7.0 copy-start.15
  134.0 7.6 copy-start.18
  134.0 8.2 copy-start.17
  160.6 116.5 %copy-start.4 = (bf16[288,384]{0,1:T(8,128)(2,1)S(1)}, bf16[288,384]{0,1:T(8,128)(2,1)}, u32[]{:S(2)}) copy-start(bf16[288,384]{0,1:T(8,128)(2,1)} %copy-done.3) | copy-start | bytes 663556
  160.6 116.5 %copy-start.9 = (bf16[384,384]{1,0:T(8,128)(2,1)S(1)}, bf16[384,384]{1,0:T(8,128)(2,1)}, u32[]{:S(2)}) copy-start(bf16[384,384]{1,0:T(8,128)(2,1)} %param.10) | copy-start | bytes 884740
  274.3 9.1 copy-start.2
  274.4 663.5 %reduce-scatter.9.cloned.1.call-start = ((), (), s32[]{:S(2)}) async-start(), calls=%async_computation.3 | async-start | bytes 221184
  277.4 22.0 %copy-start.11 = (bf16[2,6,24,384]{3,2,1,0:T(8,128)(2,1)S(1)}, bf16[2,6,24,384]{3,2,1,0:T(8,128)(2,1)}, u32[]{:S(2)}) copy-start(bf16[2,6,24,384]{3,2,1,0:T(8,128)(2,1)} %param.7) | copy-start | bytes 663556
  277.8 24.9 %copy-start.12 = (bf16[2,6,24,384]{3,2,1,0:T(8,128)(2,1)S(1)}, bf16[2,6,24,384]{3,2,1,0:T(8,128)(2,1)}, u32[]{:S(2)}) copy-start(bf16[2,6,24,384]{3,2,1,0:T(8,128)(2,1)} %param.8) | copy-start | bytes 663556
  277.8 10.3 %collective-permute-start.2 = (bf16[2,3,24,384]{3,0,2,1:T(2,128)(2,1)S(1)}, bf16[2,3,24,384]{3,0,2,1:T(2,128)(2,1)S(1)}, u32[]{:S(2)}, u32[]{:S(2)}) collective-permute-start(bf16[2,3,24,384]{3,0,2,1:T(2,128)(2,1)S(1)} %get-tuple-element.37), channel_id=1, source_target_pairs={{224,0},{0,32},{32,64},{64,96},{96,128},{128,160},{160,192},{192,2... | collective-permute-start | bytes 331784 | tf_op jit(solution)/shard_map/ppermute | solution.py:17
  285.0 6.6 collective-permute-start.6
  288.2 11.2 %collective-permute-start.3 = (bf16[2,6,6,384]{3,0,2,1:T(2,128)(2,1)S(1)}, bf16[2,6,6,384]{3,0,2,1:T(2,128)(2,1)S(1)}, u32[]{:S(2)}, u32[]{:S(2)}) collective-permute-start(bf16[2,6,6,384]{3,0,2,1:T(2,128)(2,1)S(1)} %pad_maximum_fusion.7), channel_id=1, source_target_pairs={{31,0},{0,1},{1,2},{2,3},{3,4},{4,5},{5,6},{6,7},{7,8},{8,9},{9,10... | collective-permute-start | bytes 165896 | tf_op jit(solution)/shard_map/ppermute | solution.py:17
  291.7 11.0 %collective-permute-start.7 = (bf16[2,6,6,384]{3,0,2,1:T(2,128)(2,1)S(1)}, bf16[2,6,6,384]{3,0,2,1:T(2,128)(2,1)S(1)}, u32[]{:S(2)}, u32[]{:S(2)}) collective-permute-start(bf16[2,6,6,384]{3,0,2,1:T(2,128)(2,1)S(1)} %pad_maximum_fusion.6), channel_id=1, source_target_pairs={{31,0},{0,1},{1,2},{2,3},{3,4},{4,5},{5,6},{6,7},{7,8},{8,9},{9,10... | collective-permute-start | bytes 165896 | tf_op jit(solution)/shard_map/ppermute | solution.py:17
  880.1 101.9 %reduce-scatter.7.cloned.1.call-start = ((), (), s32[]{:S(2)}) async-start(), calls=%async_computation.2 | async-start | bytes 221184
  (9 other events, 30.6 us)
Sparse Core Ops, SparseCore 0:
  274.5 603.9 all-reduce.4
  881.5 56.3 reduce-scatter.8
  940.7 41.2 reduce-scatter.6
where the time goes:
time: 993 us; the launch traced here: 990 us
  waiting for transfers between devices  679 us (68%)
  other arithmetic  131 us (13%)
  local copies, waits for them, and re-layouts  96.2 us (10%)
  starting transfers between devices  36.3 us (4%)
  matrix products  31 us (3%)
  between operations  15.6 us (2%)
    unnamed x6, waiting for transfers between devices  671 us
    scatter-add x1, other arithmetic, window_pass(): jax.ops.segment_sum(summed.T, index_table.reshape(-1), num_segments=bias_...  114 us
    gather x2, local copies, waits for them, and re-layouts, window_pass(): scores = scores + jnp.take(bias_rows, index_table, axis=1)[None]  50.3 us
    ppermute x8, starting transfers between devices, shifted(): return lax.ppermute(block, axis, route)  36.2 us
  transfers between devices with their start and end apart: 11, of which 6 were waited for; matrix products, arithmetic and copies ran while one was open for 8% of the time, Pallas kernels for 0%

commit v1 on v0

v1 whole, which is shorter than its diff:
```python
import functools
import math

import jax
import jax.numpy as jnp
import numpy as np
from jax import lax
from jax.experimental import pallas as pl
from jax.experimental.pallas import tpu as pltpu

F32 = jnp.float32
BF16 = jnp.bfloat16
HEADS = 12
WIN = 144
WIDTH = 384
POS = 3312
FACTOR = 32 ** (-0.5)


def dot(a, b):
    return lax.dot_general(a, b, (((1,), (0,)), ((), ())), preferred_element_type=F32)


def dot_nt(a, b):
    return lax.dot_general(a, b, (((1,), (1,)), ((), ())), preferred_element_type=F32)


def pack_tail(block):
    rows = []
    for q in range(3):
        parts = []
        for b in range(8):
            at = 64 * q + 8 * b
            if at < WIN:
                parts.append(block[at:at + 8, :])
            else:
                parts.append(jnp.full((8, 16), -1, block.dtype))
        rows.append(jnp.concatenate(parts, 1))
    return jnp.concatenate(rows, 0)


def compute_kernel(x_ref, c_ref, wq_ref, wp_ref, tab_ref, idx_ref, regc_ref, regr_ref,
                   branch_ref, rows_ref, g_ref, tgrad_ref,
                   tab_s, idx_s, tail_s, bias_s, qkv_s, qkvt_s, gm_s, gmt_s, mixt_s, gqt_s, gp_s,
                   unit_s, inv_s, normt_s, gs_s, acc_s):
    tab_s[...] = jnp.zeros_like(tab_s)
    tab_s[0:HEADS, 0:POS] = tab_ref[...]
    index_t = idx_ref[...].T
    idx_s[0:WIN, :] = index_t[:, 0:128]
    idx_s[WIN:168, :] = pack_tail(index_t[:, 128:144])

    def look_up(r, store):
        at = pl.multiple_of(r * 8, 8)
        entry = idx_s[pl.ds(at, 8), :]
        low = jnp.bitwise_and(entry, 127)
        high = jnp.right_shift(entry, 7)
        found = [jnp.zeros((8, 128), F32) for _ in range(HEADS)]
        for k in range(26):
            here = high == k
            for h in range(HEADS):
                line = jnp.broadcast_to(tab_s[h:h + 1, 128 * k:128 * k + 128], (8, 128))
                got = jnp.take_along_axis(line, low, axis=1, mode="promise_in_bounds")
                found[h] = jnp.where(here, got, found[h])
        for h in range(HEADS):
            store(h, at, found[h])

    def main_rows(r, carry):
        def store(h, at, value):
            bias_s[h, pl.ds(at, 8), 0:128] = value
        look_up(r, store)
        return carry

    def tail_rows(r, carry):
        def store(h, at, value):
            tail_s[h, pl.ds(pl.multiple_of(at - WIN, 8), 8), :] = value
        look_up(r, store)
        return carry

    lax.fori_loop(0, 18, main_rows, 0)
    lax.fori_loop(18, 21, tail_rows, 0)

    def spread(h, carry):
        for at in range(0, WIN, 8):
            q, b = at // 64, at % 64 // 8
            bias_s[h, at:at + 8, 128:144] = tail_s[h, 8 * q:8 * q + 8, 16 * b:16 * b + 16]
        return carry

    lax.fori_loop(0, HEADS, spread, 0)

    wq = wq_ref[...]
    wp = wp_ref[...]
    flat = x_ref[...].astype(F32)
    center = flat - jnp.mean(flat, axis=-1, keepdims=True)
    inverse = lax.rsqrt(jnp.mean(center * center, axis=-1, keepdims=True) + 1e-05)
    unit = center * inverse
    unit_s[...] = unit
    inv_s[...] = jnp.broadcast_to(inverse, inv_s.shape)
    normed = unit.astype(BF16)
    packed = dot(normed, wq).astype(BF16)
    cot = c_ref[...]
    gm_s[...] = dot_nt(cot, wp).astype(BF16)
    for w in range(2):
        at = slice(WIN * w, WIN * w + WIN)
        qkv_s[w] = packed[at]
        qkvt_s[w] = packed[at].T
        normt_s[w] = normed[at].T
        gmt_s[w] = dot_nt(wp, cot[at]).astype(BF16)

    allowed = [regc_ref[w][:, 0:1] == regr_ref[w][0:1, :] for w in range(2)]
    lane = lax.broadcasted_iota(jnp.int32, (WIN, 128), 1)
    line_of = lax.broadcasted_iota(jnp.int32, (128, WIN), 0)
    for r in range(168):
        pass
    gs_s[...] = jnp.zeros_like(gs_s)

    def group(g, carry):
        off = pl.multiple_of(g * 128, 128)
        keys = [[None] * 2 for _ in range(4)]
        grad_key = [None, None]
        grad_value = [None, None]
        for a in range(4):
            h = g * 4 + a
            mine = (line_of >= 32 * a) & (line_of < 32 * a + 32)
            mine_lane = (lane >= 32 * a) & (lane < 32 * a + 32)
            total = None
            bias = bias_s[h]
            for w in range(2):
                q = qkv_s[w, :, pl.ds(off, 128)]
                k = qkv_s[w, :, pl.ds(off + 384, 128)]
                v = qkv_s[w, :, pl.ds(off + 768, 128)]
                qt = qkvt_s[w, pl.ds(off, 128), :]
                gmt = gmt_s[w, pl.ds(off, 128), :]
                here = pl.multiple_of(off + 32 * a, 32)
                kt = qkvt_s[w, pl.ds(384 + here, 32), :]
                vt = qkvt_s[w, pl.ds(768 + here, 32), :]
                gm = gm_s[pl.ds(WIN * w, WIN), pl.ds(off, 128)]
                zero = jnp.zeros((), BF16)
                s = dot(k, jnp.where(mine, qt, zero)) * FACTOR + bias
                s = jnp.where(allowed[w], s, -1e30)
                e = jnp.exp(s - jnp.max(s, axis=0, keepdims=True))
                p = e * (1.0 / jnp.sum(e, axis=0, keepdims=True))
                pb = p.astype(BF16)
                mixt_s[w, pl.ds(here, 32), :] = dot(vt, pb).astype(BF16)
                gpr = dot(v, jnp.where(mine, gmt, zero))
                gv = dot(pb, gm)
                gs = p * (gpr - jnp.sum(p * gpr, axis=0, keepdims=True))
                sc = (gs * FACTOR).astype(BF16)
                gqt_s[w, pl.ds(here, 32), :] = dot(kt, sc).astype(BF16)
                gk = dot(sc, q)
                grad_key[w] = gk if a == 0 else jnp.where(mine_lane, gk, grad_key[w])
                grad_value[w] = gv if a == 0 else jnp.where(mine_lane, gv, grad_value[w])
                total = gs if w == 0 else total + gs
            gs_s[0:WIN, pl.ds(h, 1), :] = total[:, 0:128].reshape(WIN, 1, 128)
            gs_s[WIN:168, pl.ds(h, 1), :] = pack_tail(total[:, 128:144]).reshape(24, 1, 128)
        for w in range(2):
            rows = slice(WIN * w, WIN * w + WIN)
            gp_s[rows, pl.ds(off + 384, 128)] = grad_key[w].astype(BF16)
            gp_s[rows, pl.ds(off + 768, 128)] = grad_value[w].astype(BF16)
        return carry

    lax.fori_loop(0, 3, group, 0)

    for w in range(2):
        rows = slice(WIN * w, WIN * w + WIN)
        gp_s[rows, 0:384] = gqt_s[w].T
        branch_ref[rows, :] = dot(mixt_s[w].T, wp).astype(BF16)
    gn = dot_nt(gp_s[...], wq)
    unit = unit_s[...]
    rows_ref[...] = (inv_s[:, 0:1] * (
        gn - jnp.mean(gn, axis=-1, keepdims=True)
        - unit * jnp.mean(gn * unit, axis=-1, keepdims=True))).astype(BF16)
    for half in range(2):
        part = [dot(normt_s[w], gp_s[WIN * w:WIN * w + WIN, 576 * half:576 * half + 576]) for w in range(2)]
        g_ref[half, :, 0:576] = part[0] + part[1]
        part = [dot(mixt_s[w], c_ref[WIN * w:WIN * w + WIN, 192 * half:192 * half + 192]) for w in range(2)]
        g_ref[half, :, 576:768] = part[0] + part[1]

    acc_s[...] = jnp.zeros_like(acc_s)
    low_of = lax.broadcasted_iota(jnp.int32, (256, 128), 0)

    def pairs(r, carry):
        entry = idx_s[pl.ds(pl.multiple_of(r * 8, 8), 8), :]
        low = jnp.bitwise_and(entry, 255)
        high = jnp.right_shift(entry, 8)
        lefts = []
        rights = []
        for s in range(8):
            value = gs_s[r * 8 + s]
            lefts.append(jnp.concatenate(
                [jnp.where(high[s:s + 1, :] == k, value, 0.0).astype(BF16) for k in range(13)], 0))
            rights.append(jnp.where(low[s:s + 1, :] == low_of, 1.0, 0.0).astype(BF16))
        acc_s[...] += dot_nt(jnp.concatenate(lefts, 1), jnp.concatenate(rights, 1))
        return carry

    lax.fori_loop(0, 21, pairs, 0)
    tgrad_ref[...] = jnp.zeros_like(tgrad_ref)
    for o in range(13):
        tgrad_ref[24 * o:24 * o + 12, :] = acc_s[16 * o:16 * o + 12, 0:128]
        tgrad_ref[24 * o + 12:24 * o + 24, :] = acc_s[16 * o:16 * o + 12, 128:256]


def compute(x, c, wq, wp, tab, idx, reg):
    regc = jnp.broadcast_to(reg[:, :, None], (2, WIN, 128))
    regr = jnp.broadcast_to(reg[:, None, :], (2, 8, WIN))
    return pl.pallas_call(
        compute_kernel,
        out_shape=[
            jax.ShapeDtypeStruct((288, 384), BF16),
            jax.ShapeDtypeStruct((288, 384), BF16),
            jax.ShapeDtypeStruct((2, 384, 768), F32),
            jax.ShapeDtypeStruct((384, 128), F32),
        ],
        scratch_shapes=[
            pltpu.VMEM((16, 3328), F32),
            pltpu.VMEM((168, 128), jnp.int32),
            pltpu.VMEM((12, 24, 128), F32),
            pltpu.VMEM((12, 144, 144), F32),
            pltpu.VMEM((2, 144, 1152), BF16),
            pltpu.VMEM((2, 1152, 144), BF16),
            pltpu.VMEM((288, 384), BF16),
            pltpu.VMEM((2, 384, 144), BF16),
            pltpu.VMEM((2, 384, 144), BF16),
            pltpu.VMEM((2, 384, 144), BF16),
            pltpu.VMEM((288, 1152), BF16),
            pltpu.VMEM((288, 384), F32),
            pltpu.VMEM((288, 128), F32),
            pltpu.VMEM((2, 384, 144), BF16),
            pltpu.VMEM((168, 16, 128), F32),
            pltpu.VMEM((208, 256), F32),
        ],
        compiler_params=pltpu.CompilerParams(vmem_limit_bytes=48 * 1024 * 1024),
        name="window_math",
    )(x, c, wq, wp, tab, idx, regc, regr)


PIECES = ((0, 112), (112, 48), (160, 48))
MESH = pl.DeviceIdType.MESH


@functools.lru_cache(None)
def permutations():
    place = {}
    for l in range(2):
        for r in range(3):
            for c in range(6, 24):
                place[l, r, c] = l * 54 + r * 18 + c - 6
        for r in range(3, 6):
            for c in range(6):
                place[l, r, c] = 112 + l * 18 + (r - 3) * 6 + c
        for r in range(3):
            for c in range(6):
                place[l, r, c] = 160 + l * 18 + r * 6 + c
    send = np.zeros((208, 288), np.float32)
    for (l, r, c), at in place.items():
        send[at, l * 144 + r * 24 + c] = 1
    own = np.zeros((288, 288), np.float32)
    recv = np.zeros((288, 208), np.float32)
    for w in range(2):
        for l in range(2):
            for r in range(6):
                for c in range(12):
                    row = w * 144 + l * 72 + r * 12 + c
                    at, col = r + 3, 12 * w + c + 6
                    if at < 6 and col < 24:
                        own[row, l * 144 + at * 24 + col] = 1
                    else:
                        recv[row, place[l, at % 6, col % 24]] = 1
    return send, own, recv


def step(index, by, count):
    return lax.rem(index + (by + count), count)


def halo_in_kernel(nlat, nlon, x_ref, c_ref, take_ref, own_ref, put_ref, xo_ref, co_ref,
                   send, recv, send_sem, recv_sem):
    lat, lon = lax.axis_index("lat"), lax.axis_index("lon")
    before = [{"lat": step(lat, -1, nlat), "lon": lon}, {"lat": lat, "lon": step(lon, -1, nlon)},
              {"lat": step(lat, -1, nlat), "lon": step(lon, -1, nlon)}]
    after = [{"lat": step(lat, 1, nlat), "lon": lon}, {"lat": lat, "lon": step(lon, 1, nlon)},
             {"lat": step(lat, 1, nlat), "lon": step(lon, 1, nlon)}]
    barrier = pltpu.get_barrier_semaphore()
    for device in after:
        pl.semaphore_signal(barrier, inc=1, device_id=device, device_id_type=MESH)
    for f, ref in enumerate((x_ref, c_ref)):
        send[f] = dot(take_ref[...], ref[...]).astype(BF16)
    pl.semaphore_wait(barrier, 3)
    copies = []
    for f in range(2):
        for n, (at, size) in enumerate(PIECES):
            copy = pltpu.make_async_remote_copy(
                src_ref=send.at[f, pl.ds(at, size)], dst_ref=recv.at[f, pl.ds(at, size)],
                send_sem=send_sem.at[3 * f + n], recv_sem=recv_sem.at[3 * f + n],
                device_id=before[n], device_id_type=MESH)
            copy.start()
            copies.append(copy)
    mine = [dot(own_ref[...], ref[...]) for ref in (x_ref, c_ref)]
    for f, ref in enumerate((xo_ref, co_ref)):
        for copy in copies[3 * f:3 * f + 3]:
            copy.wait()
        ref[...] = (mine[f] + dot(put_ref[...], recv[f])).astype(BF16)


def halo_in(nlat, nlon, x, c, take, own, put):
    return pl.pallas_call(
        functools.partial(halo_in_kernel, nlat, nlon),
        out_shape=[jax.ShapeDtypeStruct((288, 384), BF16)] * 2,
        scratch_shapes=[
            pltpu.VMEM((2, 208, 384), BF16),
            pltpu.VMEM((2, 208, 384), BF16),
            pltpu.SemaphoreType.DMA((6,)),
            pltpu.SemaphoreType.DMA((6,)),
        ],
        compiler_params=pltpu.CompilerParams(
            collective_id=0, has_side_effects=True, vmem_limit_bytes=32 * 1024 * 1024),
        name="halo_in",
    )(x, c, take, own, put)


def finish_kernel(nlat, nlon, norm, x_ref, c_ref, branch_ref, rows_ref, g_ref, tpart_ref,
                  take_ref, own_ref, put_ref, xo_ref, co_ref, gq_ref, gp_ref, to_ref,
                  send, recv, gsend, gcore, lat_send, lat_recv, turn, turned, ypart, ysend, yrecv,
                  zpart, zrecv, trecv, tsum, tzrecv, tfull,
                  halo_ss, halo_rs, core_ss, core_rs, lat_ss, lat_rs, y_ss, y_rs, z_ss, z_rs,
                  t_ss, t_rs, tz_ss, tz_rs, tg_ss, tg_rs):
    nz = nlon // 8
    lev, lat, lon = lax.axis_index("lev"), lax.axis_index("lat"), lax.axis_index("lon")
    z, y = lon // 8, lax.rem(lon, 8)
    owner = lev * 8 + y

    def at_owner(o):
        return {"lev": o // 8, "lat": lat, "lon": z * 8 + lax.rem(o, 8)}

    core_peer = {"lev": 1 - lev, "lat": lat, "lon": lon}
    lat_peers = [{"lev": lev, "lat": step(lat, d, nlat), "lon": lon} for d in range(1, nlat)]
    y_peers = [{"lev": lev, "lat": lat, "lon": z * 8 + step(y, d, 8)} for d in range(1, 8)]
    z_peers = [{"lev": lev, "lat": lat, "lon": step(z, d, nz) * 8 + y} for d in range(1, nz)]
    owners = [at_owner(step(owner, d, 16)) for d in range(1, 16)]
    after = [{"lev": lev, "lat": step(lat, 1, nlat), "lon": lon},
             {"lev": lev, "lat": lat, "lon": step(lon, 1, nlon)},
             {"lev": lev, "lat": step(lat, 1, nlat), "lon": step(lon, 1, nlon)}]
    before = [{"lev": lev, "lat": lat, "lon": step(lon, -1, nlon)},
              {"lev": lev, "lat": step(lat, -1, nlat), "lon": step(lon, -1, nlon)}]
    barrier = pltpu.get_barrier_semaphore()
    greet = owners + lat_peers + z_peers + after[1:] + before
    for device in greet:
        pl.semaphore_signal(barrier, inc=1, device_id=device, device_id_type=MESH)
    gsend[...] = g_ref[1 - lev].astype(BF16)
    for f, ref in enumerate((branch_ref, rows_ref)):
        send[f] = dot(take_ref[...], ref[...]).astype(BF16)
    pl.semaphore_wait(barrier, len(greet))

    def push(src, dst, ss, rs, device):
        copy = pltpu.make_async_remote_copy(
            src_ref=src, dst_ref=dst, send_sem=ss, recv_sem=rs, device_id=device, device_id_type=MESH)
        copy.start()
        return copy

    lat_rows = [pl.ds(pl.multiple_of(48 * step(lat, d, nlat), 48), 48) for d in range(1, nlat + 1)]
    core = [push(gsend.at[rows], gcore.at[rows], core_ss.at[n], core_rs.at[n], core_peer)
            for n, rows in enumerate(lat_rows)]
    halo = [push(send.at[f, pl.ds(at, size)], recv.at[f, pl.ds(at, size)],
                 halo_ss.at[3 * f + n], halo_rs.at[3 * f + n], after[n])
            for f in range(2) for n, (at, size) in enumerate(PIECES)]
    table = [push(tpart_ref.at[pl.ds(pl.multiple_of(24 * step(owner, d, 16), 24), 24)],
                  trecv.at[d - 1], t_ss.at[d - 1], t_rs.at[d - 1], owners[d - 1])
             for d in range(1, 16)]

    over_lat = []
    for n in range(nlat - 1):
        core[n].wait()
        lat_send[n] = (g_ref[lev, lat_rows[n], :] + gcore[lat_rows[n], :].astype(F32)).astype(BF16)
        over_lat.append(push(lat_send.at[n], lat_recv.at[n], lat_ss.at[n], lat_rs.at[n], lat_peers[n]))
    core[nlat - 1].wait()
    total = g_ref[lev, lat_rows[-1], :] + gcore[lat_rows[-1], :].astype(F32)

    mine = tpart_ref[pl.ds(pl.multiple_of(24 * owner, 24), 24), :]
    for n in range(15):
        table[n].wait()
        mine = mine + trecv[n]
    tsum[0] = mine
    over_z = [push(tsum.at[0], tzrecv.at[n], tz_ss.at[n], tz_rs.at[n], z_peers[n]) for n in range(nz - 1)]

    for f, (base, ref, out) in enumerate(((x_ref, branch_ref, xo_ref), (c_ref, rows_ref, co_ref))):
        for copy in halo[3 * f:3 * f + 3]:
            copy.wait()
        rolled = dot(own_ref[...], ref[...]) + dot(put_ref[...], recv[f])
        out[...] = (base[...].astype(F32) + rolled).astype(BF16)

    for n in range(nz - 1):
        over_z[n].wait()
        mine = mine + tzrecv[n]
    tsum[1] = mine
    own_block = pl.ds(pl.multiple_of(24 * owner, 24), 24)
    gathered = [push(tsum.at[1], tfull.at[own_block], tg_ss.at[n], tg_rs.at[n], owners[n])
                for n in range(15)]

    for n in range(nlat - 1):
        over_lat[n].wait()
        total = total + lat_recv[n].astype(F32)

    turn[...] = jnp.zeros_like(turn)
    turn[0:48, :] = total
    turn[64:112, :] = total
    turned[...] = turn[...].T
    first = lax.broadcasted_iota(jnp.int32, (24, 128), 1) < 64
    for to in range(8):
        for p in range(nz // 2):
            a, b = 16 * p + to, 16 * p + 8 + to
            ypart[to, 24 * p:24 * p + 18, :] = jnp.where(
                first[0:18], turned[18 * a:18 * a + 18, :], turned[18 * b:18 * b + 18, :])
            ypart[to, 24 * p + 18:24 * p + 24, :] = jnp.where(
                first[0:6], turned[576 + 6 * a:576 + 6 * a + 6, :], turned[576 + 6 * b:576 + 6 * b + 6, :])
    ysend[...] = ypart[...].astype(BF16)
    over_y = [push(ysend.at[step(y, d, 8)], yrecv.at[d - 1], y_ss.at[d - 1], y_rs.at[d - 1], y_peers[d - 1])
              for d in range(1, 8)]
    total = ypart[y]
    for n in range(7):
        over_y[n].wait()
        total = total + yrecv[n].astype(F32)
    zpart[...] = total
    last = [push(zpart.at[pl.ds(pl.multiple_of(24 * (step(z, d, nz) // 2), 24), 24)],
                 zrecv.at[d - 1], z_ss.at[d - 1], z_rs.at[d - 1], z_peers[d - 1])
            for d in range(1, nz)]

    tfull[own_block, :] = mine
    for n in range(15):
        gathered[n].wait()
    for o in range(13):
        to_ref[:, 256 * o:256 * o + 128] = tfull[24 * o:24 * o + 12, :]
        width = min(128, POS - 256 * o - 128)
        to_ref[:, 256 * o + 128:256 * o + 128 + width] = tfull[24 * o + 12:24 * o + 24, 0:width]

    total = zpart[pl.ds(pl.multiple_of(24 * (z // 2), 24), 24), :]
    for n in range(nz - 1):
        last[n].wait()
        total = total + zrecv[n]
    total = jnp.where(lax.rem(z, 2) == 0, total[:, 0:48], total[:, 64:112]) * norm
    gq_ref[...] = total[0:18]
    gp_ref[...] = total[18:24]


def finish(nlat, nlon, norm, x, c, branch, rows, g, tpart, take, own, put):
    nz = nlon // 8
    sem = pltpu.SemaphoreType.DMA
    return pl.pallas_call(
        functools.partial(finish_kernel, nlat, nlon, norm),
        out_shape=[
            jax.ShapeDtypeStruct((288, 384), BF16),
            jax.ShapeDtypeStruct((288, 384), BF16),
            jax.ShapeDtypeStruct((18, 48), F32),
            jax.ShapeDtypeStruct((6, 48), F32),
            jax.ShapeDtypeStruct((HEADS, POS), F32),
        ],
        scratch_shapes=[
            pltpu.VMEM((2, 208, 384), BF16),
            pltpu.VMEM((2, 208, 384), BF16),
            pltpu.VMEM((384, 768), BF16),
            pltpu.VMEM((384, 768), BF16),
            pltpu.VMEM((nlat - 1, 48, 768), BF16),
            pltpu.VMEM((nlat - 1, 48, 768), BF16),
            pltpu.VMEM((128, 768), F32),
            pltpu.VMEM((768, 128), F32),
            pltpu.VMEM((8, 48, 128), F32),
            pltpu.VMEM((8, 48, 128), BF16),
            pltpu.VMEM((7, 48, 128), BF16),
            pltpu.VMEM((48, 128), F32),
            pltpu.VMEM((nz - 1, 24, 128), F32),
            pltpu.VMEM((15, 24, 128), F32),
            pltpu.VMEM((2, 24, 128), F32),
            pltpu.VMEM((nz - 1, 24, 128), F32),
            pltpu.VMEM((384, 128), F32),
            sem((6,)), sem((6,)), sem((nlat,)), sem((nlat,)), sem((nlat - 1,)), sem((nlat - 1,)),
            sem((7,)), sem((7,)), sem((nz - 1,)), sem((nz - 1,)),
            sem((15,)), sem((15,)), sem((nz - 1,)), sem((nz - 1,)), sem((15,)), sem((15,)),
        ],
        compiler_params=pltpu.CompilerParams(
            collective_id=1, has_side_effects=True, vmem_limit_bytes=48 * 1024 * 1024),
        name="finish",
    )(x, c, branch, rows, g, tpart, take, own, put)


def body(tokens, cotangent, w_qkv, w_proj, bias_table, bias_index, region_ids):
    levels, rows, columns, width = tokens.shape
    nlev, nlat, nlon = lax.axis_size("lev"), lax.axis_size("lat"), lax.axis_size("lon")
    norm = 1.0 / math.sqrt(levels * nlev * rows * nlat * columns * nlon)
    send, own, recv = permutations()
    send, own, recv, send_t, own_t, recv_t = [
        jnp.asarray(m, BF16) for m in (send, own, recv, send.T, own.T, recv.T)]
    x = tokens.reshape(288, width)
    c = cotangent.reshape(288, width)
    regions = jnp.tile(region_ids.reshape(6, 2, 12).transpose(1, 0, 2).reshape(2, 72), (1, 2))
    xw, cw = halo_in(nlat, nlon, x, c, send, own, recv)
    branch, grad_rows, g, tpart = compute(
        xw, cw, w_qkv, w_proj, bias_table[0], bias_index[0], regions)
    block_out, grad_tokens, gq, gp, table = finish(
        nlat, nlon, norm, x, c, branch, grad_rows, g, tpart, recv_t, own_t, send_t)
    return (block_out.reshape(tokens.shape), grad_tokens.reshape(tokens.shape), gq.T, gp.T, table[None])


def solution(mesh):
    return jax.shard_map(
        body,
        mesh=mesh,
        in_specs=(
            jax.P("lev", "lat", "lon", None),
            jax.P("lev", "lat", "lon", None),
            jax.P(),
            jax.P(),
            jax.P("lat", None, None),
            jax.P("lat", None, None),
            jax.P("lat", "lon"),
        ),
        out_specs=(
            jax.P("lev", "lat", "lon", None),
            jax.P("lev", "lat", "lon", None),
            jax.P("lat", ("lev", "lon")),
            jax.P("lat", ("lev", "lon")),
            jax.P("lat", None, None),
        ),
        check_vma=False,
    )
```

time: 993 us -> 103 us (0.10)
  waiting for transfers between devices: 679 us -> 0 us
  other arithmetic: 131 us -> 0 us
  Pallas kernels: 0 us -> 87.8 us
  local copies, waits for them, and re-layouts: 96.2 us -> 13.1 us
  starting transfers between devices: 36.3 us -> 0 us
  matrix products: 31 us -> 0 us
  between operations: 15.6 us -> 0.76 us
    unnamed x6 -> x0, waiting for transfers between devices: 671 us -> none
    scatter-add x1 -> x0, other arithmetic: 114 us -> none  [window_pass(): jax.ops.segment_sum(summed.T, index_table.reshape(-1), num_segments=bias_...]
    pallas_call x0 -> x3, Pallas kernels: none -> 87.8 us  [the longest x1 38.6 us: finish(): pl.pallas_call(functools.partial(finish_kernel, nlat, nlon, norm), out_sh...]
    gather x2 -> x0, local copies, waits for them, and re-layouts: 50.3 us -> none  [window_pass(): scores = scores + jnp.take(bias_rows, index_table, axis=1)[None]]
    ppermute x8 -> x0, starting transfers between devices: 36.2 us -> none  [shifted(): return lax.ppermute(block, axis, route)]
    dot_general x11 -> x0, matrix products: 26.6 us -> none  [the longest x1 6.99 us: window_pass(): jnp.einsum('bhij,bihd->bjhd', scaled, query_rows, preferred_element_type=...]
  transfers between devices with their start and end apart: 11 -> 0, of which waited for: 6 -> 0; matrix products, arithmetic and copies ran while one was open for 8% -> 0% of each run, Pallas kernels for 0% -> 0%
where the time goes in v1:
time: 103 us; the launch traced here: 102 us
  Pallas kernels  87.8 us (85%)
  local copies, waits for them, and re-layouts  13.1 us (13%)
    pallas_call x1, Pallas kernels, finish(): pl.pallas_call(functools.partial(finish_kernel, nlat, nlon, norm), out_sh...  38.6 us
    pallas_call x1, Pallas kernels, compute(): pl.pallas_call(compute_kernel, out_shape=[jax.ShapeDtypeStruct((288, 384)...  28.2 us
    pallas_call x1, Pallas kernels, halo_in(): pl.pallas_call(functools.partial(halo_in_kernel, nlat, nlon), out_shape=[...  21 us
    unnamed x32, local copies, waits for them, and re-layouts  12 us

profile of v1, /device:TPU:6, one launch (start us, length us, event | category | flops | bytes accessed | tf_op | source)
XLA Modules:
  0.0 101.6 jit_solution(522934355043475834)
XLA Ops:
  0.6 0.0 copy-start.11
  0.6 0.0 copy-start.4
  0.7 0.0 copy-start.2
  0.7 0.8 reshape.36
  1.5 0.1 tile.9
  1.6 0.1 tile.11
  1.7 0.1 broadcast_in_dim.6.regc_ref
  1.8 0.9 copy.24
  2.7 0.9 copy-done.1
  3.7 0.9 copy-done.3
  4.6 0.9 copy-done.6
  5.5 0.9 copy-done.9
  6.4 0.9 copy-done.12
  7.4 21.0 %halo_in.1 = (bf16[288,384]{1,0:T(8,128)(2,1)S(1)}, bf16[288,384]{1,0:T(8,128)(2,1)S(1)}) custom-call(bf16[288,384]{1,0:T(8,128)(2,1)S(1)} %bitcast.14, bf16[288,384]{1,0:T(8,128)(2,1)S(1)} %bitcast.16, bf16[208,288]{1,0:T(8,128)(2,1)S(1)} %copy-done.9, bf16[288,288]{1,0:T(8,128)(2,1)S(1)} %copy-done.6, bf16[288,208]{1,0:T(8,128)(2,1)S(1)} %copy-done.12), custom_call_target="tpu_custom_call" | custom-call | tf_op jit(solution)/shard_map/halo_in/pallas_call | solution.py:305
  28.3 1.2 %copy-done = bf16[384,1152]{1,0:T(8,128)(2,1)S(1)} copy-done((bf16[384,1152]{1,0:T(8,128)(2,1)S(1)}, bf16[384,1152]{1,0:T(8,128)(2,1)}, u32[]{:S(2)}) %copy-start) | copy-done | bytes 884760
  29.5 1.0 copy-done.5
  30.5 0.9 copy-done.10
  31.4 28.2 %window_math.1 = (bf16[288,384]{1,0:T(8,128)(2,1)S(1)}, bf16[288,384]{1,0:T(8,128)(2,1)S(1)}, f32[2,384,768]{2,1,0:T(8,128)S(1)}, f32[384,128]{1,0:T(8,128)S(1)}) custom-call(bf16[288,384]{1,0:T(8,128)(2,1)S(1)} %get-tuple-element.16.x_ref, bf16[288,384]{1,0:T(8,128)(2,1)S(1)} %get-tuple-element.17.c_ref, bf16[384,1152]{1,0:T(8,128)(2,1)S(1)} %copy-done, ...), custom_call_target="tpu_custom_call" | custom-call | tf_op jit(solution)/shard_map/window_math/pallas_call | solution.py:205
  59.6 38.6 %finish.1 = (bf16[288,384]{1,0:T(8,128)(2,1)S(1)}, bf16[288,384]{1,0:T(8,128)(2,1)S(1)}, f32[18,48]{1,0:T(8,128)S(1)}, f32[6,48]{1,0:T(8,128)S(1)}, f32[12,3312]{1,0:T(8,128)S(1)}) custom-call(bf16[288,384]{1,0:T(8,128)(2,1)S(1)} %bitcast.15, bf16[288,384]{1,0:T(8,128)(2,1)S(1)} %bitcast.17, bf16[288,384]{1,0:T(8,128)(2,1)S(1)} %get-tuple-element.18.branch_ref, ...), custom_call_target="tpu_custom_call" | custom-call | tf_op jit(solution)/shard_map/finish/pallas_call | solution.py:446
  98.2 0.8 copy.20
  99.1 0.7 copy.30
  99.8 0.7 copy.31
  100.4 0.6 copy.32
  101.0 0.6 copy.33
  (18 shorter events, 0.0 us)
Async XLA Ops:
  0.6 58.9 %copy-start.11 = (bf16[288,208]{1,0:T(8,128)(2,1)S(1)}, bf16[288,208]{1,0:T(8,128)(2,1)}, u32[]{:S(2)}) copy-start(bf16[288,208]{1,0:T(8,128)(2,1)} %constant.15.clone.put_ref) | copy-start | bytes 359428
  0.6 58.9 %copy-start.4 = (bf16[2,6,24,384]{3,2,1,0:T(8,128)(2,1)S(1)}, bf16[2,6,24,384]{3,2,1,0:T(8,128)(2,1)}, u32[]{:S(2)}) copy-start(bf16[2,6,24,384]{3,2,1,0:T(8,128)(2,1)} %param.14) | copy-start | bytes 663556
  0.7 58.9 %copy-start.2 = (bf16[2,6,24,384]{3,2,1,0:T(8,128)(2,1)S(1)}, bf16[2,6,24,384]{3,2,1,0:T(8,128)(2,1)}, u32[]{:S(2)}) copy-start(bf16[2,6,24,384]{3,2,1,0:T(8,128)(2,1)} %param.13) | copy-start | bytes 663556
  2.7 0.9 copy-start.1
  3.7 0.9 copy-start.3
  4.6 0.9 copy-start.6
  5.5 0.9 copy-start.9
  6.4 0.9 copy-start.12
  7.4 52.2 %copy-start.7 = (bf16[288,288]{1,0:T(8,128)(2,1)S(1)}, bf16[288,288]{1,0:T(8,128)(2,1)}, u32[]{:S(2)}) copy-start(bf16[288,288]{1,0:T(8,128)(2,1)} %constant.16.clone.own_ref) | copy-start | bytes 497668
  7.4 52.2 %copy-start.8 = (bf16[208,288]{1,0:T(8,128)(2,1)S(1)}, bf16[208,288]{1,0:T(8,128)(2,1)}, u32[]{:S(2)}) copy-start(bf16[208,288]{1,0:T(8,128)(2,1)} %constant.17.clone.take_ref) | copy-start | bytes 359428
  28.3 1.2 %copy-start = (bf16[384,1152]{1,0:T(8,128)(2,1)S(1)}, bf16[384,1152]{1,0:T(8,128)(2,1)}, u32[]{:S(2)}) copy-start(bf16[384,1152]{1,0:T(8,128)(2,1)} %wq_ref.1) | copy-start | bytes 2654212
  29.5 1.0 copy-start.5
  30.5 0.9 copy-start.10

commit v2 on v0

v2 whole, which is shorter than its diff:
```python
import functools
import math

import jax
import jax.numpy as jnp
import numpy as np
from jax import lax
from jax.experimental import pallas as pl
from jax.experimental.pallas import tpu as pltpu

F32 = jnp.float32
BF16 = jnp.bfloat16
HEADS = 12
WIN = 144
WIDTH = 384
POS = 3312
FACTOR = 32 ** (-0.5)


def dot(a, b):
    return lax.dot_general(a, b, (((1,), (0,)), ((), ())), preferred_element_type=F32)


def dot_nt(a, b):
    return lax.dot_general(a, b, (((1,), (1,)), ((), ())), preferred_element_type=F32)


def pack_tail(block):
    rows = []
    for q in range(3):
        parts = []
        for b in range(8):
            at = 64 * q + 8 * b
            if at < WIN:
                parts.append(block[at:at + 8, :])
            else:
                parts.append(jnp.full((8, 16), -1, block.dtype))
        rows.append(jnp.concatenate(parts, 1))
    return jnp.concatenate(rows, 0)


PIECES = ((0, 112), (112, 48), (160, 48))
MESH = pl.DeviceIdType.MESH


@functools.lru_cache(None)
def permutations():
    place = {}
    for l in range(2):
        for r in range(3):
            for c in range(6, 24):
                place[l, r, c] = l * 54 + r * 18 + c - 6
        for r in range(3, 6):
            for c in range(6):
                place[l, r, c] = 112 + l * 18 + (r - 3) * 6 + c
        for r in range(3):
            for c in range(6):
                place[l, r, c] = 160 + l * 18 + r * 6 + c
    send = np.zeros((208, 288), np.float32)
    for (l, r, c), at in place.items():
        send[at, l * 144 + r * 24 + c] = 1
    own = np.zeros((288, 288), np.float32)
    recv = np.zeros((288, 208), np.float32)
    for w in range(2):
        for l in range(2):
            for r in range(6):
                for c in range(12):
                    row = w * 144 + l * 72 + r * 12 + c
                    at, col = r + 3, 12 * w + c + 6
                    if at < 6 and col < 24:
                        own[row, l * 144 + at * 24 + col] = 1
                    else:
                        recv[row, place[l, at % 6, col % 24]] = 1
    return send, own, recv


def step(index, by, count):
    return lax.rem(index + (by + count), count)


def block_kernel(nlat, nlon, norm, x_hbm, c_hbm, wq_hbm, wp_hbm, tab_hbm, idx_hbm, reg_hbm,
                 take_hbm, own_hbm, put_hbm, take_t_hbm, own_t_hbm, put_t_hbm,
                 xo_ref, co_ref, gq_ref, gp_ref, to_ref,
                 x_ref, c_ref, wq_ref, wp_ref, tab_ref, idx_ref, reg_ref,
                 take_ref, own_ref, put_ref, take_t_ref, own_t_ref, put_t_ref,
                 xw_s, cw_s, idx_s, tail_s, bias_s, qkv_s, qkvt_s, gm_s, gmt_s, mixt_s, gqt_s, gp_s,
                 unit_s, inv_s, normt_s, gs_s, acc_s, branch_s, rows_s, g_s, tpart,
                 send_in, recv_in, send, recv, gsend, gcore, lat_send, lat_recv, turn, turned, ypart, ysend, yrecv,
                 zpart, zrecv, trecv, tsum, tzrecv, tfull,
                 load_sem, in_ss, in_rs, halo_ss, halo_rs, core_ss, core_rs, lat_ss, lat_rs,
                 y_ss, y_rs, z_ss, z_rs, t_ss, t_rs, tz_ss, tz_rs, tg_ss, tg_rs):
    names = ("x", "c", "take", "own", "put", "tab", "idx", "reg", "wq", "wp", "own_t", "take_t", "put_t")
    from_to = ((x_hbm, x_ref), (c_hbm, c_ref), (take_hbm, take_ref), (own_hbm, own_ref), (put_hbm, put_ref),
                (tab_hbm, tab_ref), (idx_hbm, idx_ref), (reg_hbm, reg_ref), (wq_hbm, wq_ref), (wp_hbm, wp_ref),
                (own_t_hbm, own_t_ref), (take_t_hbm, take_t_ref), (put_t_hbm, put_t_ref))
    loads = {}
    for n, (name, (src, dst)) in enumerate(zip(names, from_to)):
        loads[name] = pltpu.make_async_copy(src, dst, load_sem.at[n])
        loads[name].start()

    nz = nlon // 8
    lev, lat, lon = lax.axis_index("lev"), lax.axis_index("lat"), lax.axis_index("lon")
    z, y = lon // 8, lax.rem(lon, 8)
    owner = lev * 8 + y

    def at_owner(o):
        return {"lev": o // 8, "lat": lat, "lon": z * 8 + lax.rem(o, 8)}

    core_peer = {"lev": 1 - lev, "lat": lat, "lon": lon}
    lat_peers = [{"lev": lev, "lat": step(lat, d, nlat), "lon": lon} for d in range(1, nlat)]
    y_peers = [{"lev": lev, "lat": lat, "lon": z * 8 + step(y, d, 8)} for d in range(1, 8)]
    z_peers = [{"lev": lev, "lat": lat, "lon": step(z, d, nz) * 8 + y} for d in range(1, nz)]
    owners = [at_owner(step(owner, d, 16)) for d in range(1, 16)]
    after, before = [
        [{"lev": lev, "lat": step(lat, by, nlat), "lon": lon},
         {"lev": lev, "lat": lat, "lon": step(lon, by, nlon)},
         {"lev": lev, "lat": step(lat, by, nlat), "lon": step(lon, by, nlon)}] for by in (1, -1)]
    barrier = pltpu.get_barrier_semaphore()
    greet = after[1:] + before[1:] + lat_peers + owners + z_peers
    for device in greet:
        pl.semaphore_signal(barrier, inc=1, device_id=device, device_id_type=MESH)

    def push(src, dst, ss, rs, device):
        copy = pltpu.make_async_remote_copy(
            src_ref=src, dst_ref=dst, send_sem=ss, recv_sem=rs, device_id=device, device_id_type=MESH)
        copy.start()
        return copy

    for name in ("x", "c", "take"):
        loads[name].wait()
    for f, ref in enumerate((x_ref, c_ref)):
        send_in[f] = dot(take_ref[...], ref[...]).astype(BF16)
    pl.semaphore_wait(barrier, len(greet))
    arrive = [push(send_in.at[f, pl.ds(at, size)], recv_in.at[f, pl.ds(at, size)],
                   in_ss.at[3 * f + n], in_rs.at[3 * f + n], before[n])
              for f in range(2) for n, (at, size) in enumerate(PIECES)]

    for name in ("tab", "idx"):
        loads[name].wait()
    index_t = idx_ref[...].T
    idx_s[0:WIN, :] = index_t[:, 0:128]
    idx_s[WIN:168, :] = pack_tail(index_t[:, 128:144])

    def look_up(r, store):
        at = pl.multiple_of(r * 8, 8)
        entry = idx_s[pl.ds(at, 8), :]
        low = jnp.bitwise_and(entry, 127)
        high = jnp.right_shift(entry, 7)
        found = [jnp.zeros((8, 128), F32) for _ in range(HEADS)]
        for k in range(26):
            here = high == k
            width = min(128, POS - 128 * k)
            for h in range(HEADS):
                line = tab_ref[h, 0:1, 128 * k:128 * k + width]
                if width < 128:
                    line = jnp.concatenate([line, jnp.zeros((1, 128 - width), F32)], 1)
                line = jnp.broadcast_to(line, (8, 128))
                got = jnp.take_along_axis(line, low, axis=1, mode="promise_in_bounds")
                found[h] = jnp.where(here, got, found[h])
        for h in range(HEADS):
            store(h, at, found[h])

    def main_rows(r, carry):
        def store(h, at, value):
            bias_s[h, pl.ds(at, 8), 0:128] = value
        look_up(r, store)
        return carry

    def tail_rows(r, carry):
        def store(h, at, value):
            tail_s[h, pl.ds(pl.multiple_of(at - WIN, 8), 8), :] = value
        look_up(r, store)
        return carry

    lax.fori_loop(0, 18, main_rows, 0)
    lax.fori_loop(18, 21, tail_rows, 0)

    def spread(h, carry):
        for at in range(0, WIN, 8):
            q, b = at // 64, at % 64 // 8
            bias_s[h, at:at + 8, 128:144] = tail_s[h, 8 * q:8 * q + 8, 16 * b:16 * b + 16]
        return carry

    lax.fori_loop(0, HEADS, spread, 0)
    gs_s[...] = jnp.zeros_like(gs_s)

    loads["reg"].wait()
    region = reg_ref[...].astype(F32).astype(BF16)
    col_of = lax.broadcasted_iota(jnp.int32, (24, WIN), 0)
    place = lax.broadcasted_iota(jnp.int32, (24, WIN), 1)
    row_of = lax.broadcasted_iota(jnp.int32, (6, WIN), 0)
    row_at = lax.rem(lax.broadcasted_iota(jnp.int32, (6, WIN), 1), 72) // 12
    allowed = []
    for w in range(2):
        choose = jnp.where(col_of == lax.rem(place, 12) + 12 * w, 1.0, 0.0).astype(BF16)
        line = jnp.sum(jnp.where(row_of == row_at, dot(region, choose), 0.0), axis=0, keepdims=True)
        down = jnp.broadcast_to(line, (128, WIN)).T
        allowed.append(down[:, 0:1] == line)

    loads["own"].wait()
    loads["put"].wait()
    mine = [dot(own_ref[...], ref[...]) for ref in (x_ref, c_ref)]
    for f, ref in enumerate((xw_s, cw_s)):
        for copy in arrive[3 * f:3 * f + 3]:
            copy.wait()
        ref[...] = (mine[f] + dot(put_ref[...], recv_in[f])).astype(BF16)

    loads["wq"].wait()
    loads["wp"].wait()
    flat = xw_s[...].astype(F32)
    center = flat - jnp.mean(flat, axis=-1, keepdims=True)
    inverse = lax.rsqrt(jnp.mean(center * center, axis=-1, keepdims=True) + 1e-05)
    unit = center * inverse
    unit_s[...] = unit
    inv_s[...] = jnp.broadcast_to(inverse, inv_s.shape)
    normed = unit.astype(BF16)
    packed = dot(normed, wq_ref[...]).astype(BF16)
    cot = cw_s[...]
    gm_s[...] = dot_nt(cot, wp_ref[...]).astype(BF16)
    for w in range(2):
        at = slice(WIN * w, WIN * w + WIN)
        qkv_s[w] = packed[at]
        qkvt_s[w] = packed[at].T
        normt_s[w] = normed[at].T
        gmt_s[w] = dot_nt(wp_ref[...], cot[at]).astype(BF16)

    lane = lax.broadcasted_iota(jnp.int32, (WIN, 128), 1)
    line_of = lax.broadcasted_iota(jnp.int32, (128, WIN), 0)

    def group(g, carry):
        off = pl.multiple_of(g * 128, 128)
        grad_key = [None, None]
        grad_value = [None, None]
        for a in range(4):
            h = g * 4 + a
            own_line = (line_of >= 32 * a) & (line_of < 32 * a + 32)
            own_lane = (lane >= 32 * a) & (lane < 32 * a + 32)
            total = None
            bias = bias_s[h]
            for w in range(2):
                q = qkv_s[w, :, pl.ds(off, 128)]
                k = qkv_s[w, :, pl.ds(off + 384, 128)]
                v = qkv_s[w, :, pl.ds(off + 768, 128)]
                qt = qkvt_s[w, pl.ds(off, 128), :]
                gmt = gmt_s[w, pl.ds(off, 128), :]
                here = pl.multiple_of(off + 32 * a, 32)
                kt = qkvt_s[w, pl.ds(384 + here, 32), :]
                vt = qkvt_s[w, pl.ds(768 + here, 32), :]
                gm = gm_s[pl.ds(WIN * w, WIN), pl.ds(off, 128)]
                zero = jnp.zeros((), BF16)
                s = dot(k, jnp.where(own_line, qt, zero)) * FACTOR + bias
                s = jnp.where(allowed[w], s, -1e30)
                e = jnp.exp(s - jnp.max(s, axis=0, keepdims=True))
                p = e * (1.0 / jnp.sum(e, axis=0, keepdims=True))
                pb = p.astype(BF16)
                mixt_s[w, pl.ds(here, 32), :] = dot(vt, pb).astype(BF16)
                gpr = dot(v, jnp.where(own_line, gmt, zero))
                gv = dot(pb, gm)
                gs = p * (gpr - jnp.sum(p * gpr, axis=0, keepdims=True))
                sc = (gs * FACTOR).astype(BF16)
                gqt_s[w, pl.ds(here, 32), :] = dot(kt, sc).astype(BF16)
                gk = dot(sc, q)
                grad_key[w] = gk if a == 0 else jnp.where(own_lane, gk, grad_key[w])
                grad_value[w] = gv if a == 0 else jnp.where(own_lane, gv, grad_value[w])
                total = gs if w == 0 else total + gs
            gs_s[0:WIN, pl.ds(h, 1), :] = total[:, 0:128].reshape(WIN, 1, 128)
            gs_s[WIN:168, pl.ds(h, 1), :] = pack_tail(total[:, 128:144]).reshape(24, 1, 128)
        for w in range(2):
            rows = slice(WIN * w, WIN * w + WIN)
            gp_s[rows, pl.ds(off + 384, 128)] = grad_key[w].astype(BF16)
            gp_s[rows, pl.ds(off + 768, 128)] = grad_value[w].astype(BF16)
        return carry

    lax.fori_loop(0, 3, group, 0)

    for w in range(2):
        gp_s[WIN * w:WIN * w + WIN, 0:384] = gqt_s[w].T
    for half in range(2):
        part = [dot(normt_s[w], gp_s[WIN * w:WIN * w + WIN, 576 * half:576 * half + 576]) for w in range(2)]
        g_s[half, :, 0:576] = part[0] + part[1]
        part = [dot(mixt_s[w], cw_s[WIN * w:WIN * w + WIN, 192 * half:192 * half + 192]) for w in range(2)]
        g_s[half, :, 576:768] = part[0] + part[1]
    gsend[...] = g_s[1 - lev].astype(BF16)
    lat_rows = [pl.ds(pl.multiple_of(48 * step(lat, d, nlat), 48), 48) for d in range(1, nlat + 1)]
    core = [push(gsend.at[rows], gcore.at[rows], core_ss.at[n], core_rs.at[n], core_peer)
            for n, rows in enumerate(lat_rows)]

    loads["put_t"].wait()
    halo = []

    def halo_out(f, ref):
        send[f] = dot(put_t_ref[...], ref[...]).astype(BF16)
        for n, (at, size) in enumerate(PIECES):
            halo.append(push(send.at[f, pl.ds(at, size)], recv.at[f, pl.ds(at, size)],
                             halo_ss.at[3 * f + n], halo_rs.at[3 * f + n], after[n]))

    for w in range(2):
        branch_s[WIN * w:WIN * w + WIN, :] = dot(mixt_s[w].T, wp_ref[...]).astype(BF16)
    halo_out(0, branch_s)

    over_lat = []
    for n in range(nlat - 1):
        core[n].wait()
        lat_send[n] = (g_s[lev, lat_rows[n], :] + gcore[lat_rows[n], :].astype(F32)).astype(BF16)
        over_lat.append(push(lat_send.at[n], lat_recv.at[n], lat_ss.at[n], lat_rs.at[n], lat_peers[n]))
    core[nlat - 1].wait()

    gn = dot_nt(gp_s[...], wq_ref[...])
    unit = unit_s[...]
    rows_s[...] = (inv_s[:, 0:1] * (
        gn - jnp.mean(gn, axis=-1, keepdims=True)
        - unit * jnp.mean(gn * unit, axis=-1, keepdims=True))).astype(BF16)
    halo_out(1, rows_s)

    acc_s[...] = jnp.zeros_like(acc_s)
    low_of = lax.broadcasted_iota(jnp.int32, (256, 128), 0)

    def pairs(r, carry):
        entry = idx_s[pl.ds(pl.multiple_of(r * 8, 8), 8), :]
        low = jnp.bitwise_and(entry, 255)
        high = jnp.right_shift(entry, 8)
        lefts = []
        rights = []
        for s in range(8):
            value = gs_s[r * 8 + s]
            lefts.append(jnp.concatenate(
                [jnp.where(high[s:s + 1, :] == k, value, 0.0).astype(BF16) for k in range(13)], 0))
            rights.append(jnp.where(low[s:s + 1, :] == low_of, 1.0, 0.0).astype(BF16))
        acc_s[...] += dot_nt(jnp.concatenate(lefts, 1), jnp.concatenate(rights, 1))
        return carry

    lax.fori_loop(0, 21, pairs, 0)
    tpart[...] = jnp.zeros_like(tpart)
    for o in range(13):
        tpart[24 * o:24 * o + 12, :] = acc_s[16 * o:16 * o + 12, 0:128]
        tpart[24 * o + 12:24 * o + 24, :] = acc_s[16 * o:16 * o + 12, 128:256]
    table = [push(tpart.at[pl.ds(pl.multiple_of(24 * step(owner, d, 16), 24), 24)],
                  trecv.at[d - 1], t_ss.at[d - 1], t_rs.at[d - 1], owners[d - 1])
             for d in range(1, 16)]

    total = g_s[lev, lat_rows[-1], :] + gcore[lat_rows[-1], :].astype(F32)
    for n in range(nlat - 1):
        over_lat[n].wait()
        total = total + lat_recv[n].astype(F32)
    turn[...] = jnp.zeros_like(turn)
    turn[0:48, :] = total
    turn[64:112, :] = total
    turned[...] = turn[...].T
    first = lax.broadcasted_iota(jnp.int32, (24, 128), 1) < 64
    for to in range(8):
        for p in range(nz // 2):
            a, b = 16 * p + to, 16 * p + 8 + to
            ypart[to, 24 * p:24 * p + 18, :] = jnp.where(
                first[0:18], turned[18 * a:18 * a + 18, :], turned[18 * b:18 * b + 18, :])
            ypart[to, 24 * p + 18:24 * p + 24, :] = jnp.where(
                first[0:6], turned[576 + 6 * a:576 + 6 * a + 6, :], turned[576 + 6 * b:576 + 6 * b + 6, :])
    ysend[...] = ypart[...].astype(BF16)
    over_y = [push(ysend.at[step(y, d, 8)], yrecv.at[d - 1], y_ss.at[d - 1], y_rs.at[d - 1], y_peers[d - 1])
              for d in range(1, 8)]

    own_block = pl.ds(pl.multiple_of(24 * owner, 24), 24)
    part = tpart[own_block, :]
    for n in range(15):
        table[n].wait()
        part = part + trecv[n]
    tsum[0] = part
    over_z = [push(tsum.at[0], tzrecv.at[n], tz_ss.at[n], tz_rs.at[n], z_peers[n]) for n in range(nz - 1)]

    total = ypart[y]
    for n in range(7):
        over_y[n].wait()
        total = total + yrecv[n].astype(F32)
    zpart[...] = total
    last = [push(zpart.at[pl.ds(pl.multiple_of(24 * (step(z, d, nz) // 2), 24), 24)],
                 zrecv.at[d - 1], z_ss.at[d - 1], z_rs.at[d - 1], z_peers[d - 1])
            for d in range(1, nz)]

    for n in range(nz - 1):
        over_z[n].wait()
        part = part + tzrecv[n]
    tsum[1] = part
    gathered = [push(tsum.at[1], tfull.at[own_block], tg_ss.at[n], tg_rs.at[n], owners[n])
                for n in range(15)]

    loads["own_t"].wait()
    loads["take_t"].wait()
    for f, (base, ref, out) in enumerate(((x_ref, branch_s, xo_ref), (c_ref, rows_s, co_ref))):
        for copy in halo[3 * f:3 * f + 3]:
            copy.wait()
        rolled = dot(own_t_ref[...], ref[...]) + dot(take_t_ref[...], recv[f])
        out[...] = (base[...].astype(F32) + rolled).astype(BF16)

    total = zpart[pl.ds(pl.multiple_of(24 * (z // 2), 24), 24), :]
    for n in range(nz - 1):
        last[n].wait()
        total = total + zrecv[n]
    total = jnp.where(lax.rem(z, 2) == 0, total[:, 0:48], total[:, 64:112]) * norm
    gq_ref[...] = total[0:18]
    gp_ref[...] = total[18:24]

    tfull[own_block, :] = part
    for n in range(15):
        gathered[n].wait()
    for o in range(13):
        width = min(128, POS - 256 * o - 128)
        for h in range(HEADS):
            to_ref[h, :, 256 * o:256 * o + 128] = tfull[24 * o + h:24 * o + h + 1, :]
            to_ref[h, :, 256 * o + 128:256 * o + 128 + width] = tfull[24 * o + 12 + h:24 * o + 13 + h, 0:width]


def block(nlat, nlon, norm, *operands):
    nz = nlon // 8
    sem = pltpu.SemaphoreType.DMA
    vmem = pltpu.VMEM
    loaded = [operands[n] for n in range(13)]
    return pl.pallas_call(
        functools.partial(block_kernel, nlat, nlon, norm),
        in_specs=[pl.BlockSpec(memory_space=pl.ANY)] * 13,
        out_shape=[
            jax.ShapeDtypeStruct((288, 384), BF16),
            jax.ShapeDtypeStruct((288, 384), BF16),
            jax.ShapeDtypeStruct((18, 48), F32),
            jax.ShapeDtypeStruct((6, 48), F32),
            jax.ShapeDtypeStruct((HEADS, 1, POS), F32),
        ],
        scratch_shapes=[vmem(a.shape, a.dtype) for a in loaded] + [
            vmem((288, 384), BF16),
            vmem((288, 384), BF16),
            vmem((168, 128), jnp.int32),
            vmem((12, 24, 128), F32),
            vmem((12, 144, 144), F32),
            vmem((2, 144, 1152), BF16),
            vmem((2, 1152, 144), BF16),
            vmem((288, 384), BF16),
            vmem((2, 384, 144), BF16),
            vmem((2, 384, 144), BF16),
            vmem((2, 384, 144), BF16),
            vmem((288, 1152), BF16),
            vmem((288, 384), F32),
            vmem((288, 128), F32),
            vmem((2, 384, 144), BF16),
            vmem((168, 16, 128), F32),
            vmem((208, 256), F32),
            vmem((288, 384), BF16),
            vmem((288, 384), BF16),
            vmem((2, 384, 768), F32),
            vmem((384, 128), F32),
            vmem((2, 208, 384), BF16),
            vmem((2, 208, 384), BF16),
            vmem((2, 208, 384), BF16),
            vmem((2, 208, 384), BF16),
            vmem((384, 768), BF16),
            vmem((384, 768), BF16),
            vmem((nlat - 1, 48, 768), BF16),
            vmem((nlat - 1, 48, 768), BF16),
            vmem((128, 768), F32),
            vmem((768, 128), F32),
            vmem((8, 48, 128), F32),
            vmem((8, 48, 128), BF16),
            vmem((7, 48, 128), BF16),
            vmem((48, 128), F32),
            vmem((nz - 1, 24, 128), F32),
            vmem((15, 24, 128), F32),
            vmem((2, 24, 128), F32),
            vmem((nz - 1, 24, 128), F32),
            vmem((384, 128), F32),
            sem((13,)), sem((6,)), sem((6,)), sem((6,)), sem((6,)), sem((nlat,)), sem((nlat,)),
            sem((nlat - 1,)), sem((nlat - 1,)),
            sem((7,)), sem((7,)), sem((nz - 1,)), sem((nz - 1,)),
            sem((15,)), sem((15,)), sem((nz - 1,)), sem((nz - 1,)), sem((15,)), sem((15,)),
        ],
        compiler_params=pltpu.CompilerParams(
            collective_id=0, has_side_effects=True, vmem_limit_bytes=56 * 1024 * 1024),
        name="block",
    )(*operands)


def publish_kernel(*refs):
    sems = refs[-1]
    copies = [pltpu.make_async_copy(refs[n], refs[5 + n], sems.at[n]) for n in range(5)]
    for copy in copies:
        copy.start()
    for copy in copies:
        copy.wait()


def publish(*results):
    return pl.pallas_call(
        publish_kernel,
        in_specs=[pl.BlockSpec(memory_space=pl.ANY)] * 5,
        out_specs=[pl.BlockSpec(memory_space=pl.ANY)] * 5,
        out_shape=[jax.ShapeDtypeStruct(r.shape, r.dtype) for r in results],
        scratch_shapes=[pltpu.SemaphoreType.DMA((5,))],
        name="publish",
    )(*results)


def body(tokens, cotangent, w_qkv, w_proj, bias_table, bias_index, region_ids):
    levels, rows, columns, width = tokens.shape
    nlev, nlat, nlon = lax.axis_size("lev"), lax.axis_size("lat"), lax.axis_size("lon")
    norm = 1.0 / math.sqrt(levels * nlev * rows * nlat * columns * nlon)
    send, own, recv = permutations()
    send, own, recv, send_t, own_t, recv_t = [
        jnp.asarray(m, BF16) for m in (send, own, recv, send.T, own.T, recv.T)]
    results = block(
        nlat, nlon, norm, tokens.reshape(288, width), cotangent.reshape(288, width), w_qkv, w_proj,
        bias_table.transpose(1, 0, 2), bias_index[0], region_ids, send, own, recv, send_t, own_t, recv_t)
    block_out, grad_tokens, gq, gp, table = publish(*results)
    return (block_out.reshape(tokens.shape), grad_tokens.reshape(tokens.shape), gq.T, gp.T,
            table.transpose(1, 0, 2))


def solution(mesh):
    return jax.shard_map(
        body,
        mesh=mesh,
        in_specs=(
            jax.P("lev", "lat", "lon", None),
            jax.P("lev", "lat", "lon", None),
            jax.P(),
            jax.P(),
            jax.P("lat", None, None),
            jax.P("lat", None, None),
            jax.P("lat", "lon"),
        ),
        out_specs=(
            jax.P("lev", "lat", "lon", None),
            jax.P("lev", "lat", "lon", None),
            jax.P("lat", ("lev", "lon")),
            jax.P("lat", ("lev", "lon")),
            jax.P("lat", None, None),
        ),
        check_vma=False,
    )
```

time: 993 us -> 87.8 us (0.09)
  the two profiles are of different devices: /device:TPU:6 before, /device:TPU:4 now
where the time goes in v2:
time: 87.8 us; the launch traced here: 87.7 us
  Pallas kernels  87 us (99%)
    pallas_call x1, Pallas kernels, block(): pl.pallas_call(functools.partial(block_kernel, nlat, nlon, norm), in_spec...  67.3 us
    pallas_call x1, Pallas kernels, publish(): pl.pallas_call(publish_kernel, in_specs=[pl.BlockSpec(memory_space=pl.ANY...  19.8 us

profile of v2, /device:TPU:4, one launch (start us, length us, event | category | flops | bytes accessed | tf_op | source)
XLA Modules:
  0.0 87.7 jit_solution(9189983129611898507)
XLA Ops:
  0.6 67.3 %block.1 = (bf16[288,384]{1,0:T(8,128)(2,1)}, bf16[288,384]{1,0:T(8,128)(2,1)}, f32[18,48]{1,0:T(8,128)}, f32[6,48]{1,0:T(8,128)}, f32[12,1,3312]{2,1,0:T(1,128)}) custom-call(bf16[288,384]{1,0:T(8,128)(2,1)} %bitcast.9, bf16[288,384]{1,0:T(8,128)(2,1)} %bitcast.10, bf16[384,1152]{1,0:T(8,128)(2,1)} %wq_hbm.1, bf16[384,384]{1,0:T(8,128)(2,1)} %wp_hbm.1, ...), custom_call_target="tpu_custom_call" | custom-call | tf_op jit(solution)/shard_map/block/pallas_call | solution.py:416
  67.9 19.8 %publish.1 = (bf16[288,384]{1,0:T(8,128)(2,1)}, bf16[288,384]{1,0:T(8,128)(2,1)}, f32[18,48]{1,0:T(8,128)}, f32[6,48]{1,0:T(8,128)}, f32[12,1,3312]{2,1,0:T(1,128)}) custom-call(bf16[288,384]{1,0:T(8,128)(2,1)} %get-tuple-element.15.refs_0_, bf16[288,384]{1,0:T(8,128)(2,1)} %get-tuple-element.16.refs_1_, f32[18,48]{1,0:T(8,128)} %get-tuple-element.17.refs_2_, ...), custom_call_target="tpu_custom_call" | custom-call | tf_op jit(solution)/shard_map/publish/pallas_call | solution.py:488

commit v3 on v2

--- a/solution.py
+++ b/solution.py
@@ -14,6 +14,7 @@
 WIN = 144
 WIDTH = 384
 POS = 3312
+GRAIN = 32767 / 5
 FACTOR = 32 ** (-0.5)
 
 
@@ -83,7 +84,7 @@
                  xo_ref, co_ref, gq_ref, gp_ref, to_ref,
                  x_ref, c_ref, wq_ref, wp_ref, tab_ref, idx_ref, reg_ref,
                  take_ref, own_ref, put_ref, take_t_ref, own_t_ref, put_t_ref,
-                 xw_s, cw_s, idx_s, tail_s, bias_s, qkv_s, qkvt_s, gm_s, gmt_s, mixt_s, gqt_s, gp_s,
+                 xw_s, cw_s, words_s, rows_of_table, idx_s, tail_s, bias_s, qkv_s, qkvt_s, gm_s, gmt_s, mixt_s, gqt_s, gp_s,
                  unit_s, inv_s, normt_s, gs_s, acc_s, branch_s, rows_s, g_s, tpart,
                  send_in, recv_in, send, recv, gsend, gcore, lat_send, lat_recv, turn, turned, ypart, ysend, yrecv,
                  zpart, zrecv, trecv, tsum, tzrecv, tfull,
@@ -137,6 +138,12 @@
 
     for name in ("tab", "idx"):
         loads[name].wait()
+    words_s[...] = jnp.zeros_like(words_s)
+    for h in range(HEADS):
+        rows_of_table[h:h + 1, :] = tab_ref[h]
+    upper = jnp.floor(rows_of_table[0:6, :] * GRAIN + 0.5).astype(jnp.int32)
+    lower = jnp.floor(rows_of_table[6:12, :] * GRAIN + 0.5).astype(jnp.int32)
+    words_s[0:6, 0:POS] = jnp.left_shift(upper, 16) + jnp.bitwise_and(lower, 65535)
     index_t = idx_ref[...].T
     idx_s[0:WIN, :] = index_t[:, 0:128]
     idx_s[WIN:168, :] = pack_tail(index_t[:, 128:144])
@@ -146,19 +153,17 @@
         entry = idx_s[pl.ds(at, 8), :]
         low = jnp.bitwise_and(entry, 127)
         high = jnp.right_shift(entry, 7)
-        found = [jnp.zeros((8, 128), F32) for _ in range(HEADS)]
+        found = [jnp.zeros((8, 128), jnp.int32) for _ in range(6)]
         for k in range(26):
             here = high == k
-            width = min(128, POS - 128 * k)
-            for h in range(HEADS):
-                line = tab_ref[h, 0:1, 128 * k:128 * k + width]
-                if width < 128:
-                    line = jnp.concatenate([line, jnp.zeros((1, 128 - width), F32)], 1)
-                line = jnp.broadcast_to(line, (8, 128))
+            for h in range(6):
+                line = jnp.broadcast_to(words_s[h:h + 1, 128 * k:128 * k + 128], (8, 128))
                 got = jnp.take_along_axis(line, low, axis=1, mode="promise_in_bounds")
                 found[h] = jnp.where(here, got, found[h])
-        for h in range(HEADS):
-            store(h, at, found[h])
+        for h in range(6):
+            store(h, at, jnp.right_shift(found[h], 16).astype(F32) * (1 / GRAIN))
+            half = jnp.right_shift(jnp.left_shift(found[h], 16), 16)
+            store(h + 6, at, half.astype(F32) * (1 / GRAIN))
 
     def main_rows(r, carry):
         def store(h, at, value):
@@ -200,10 +205,13 @@
     loads["own"].wait()
     loads["put"].wait()
     mine = [dot(own_ref[...], ref[...]) for ref in (x_ref, c_ref)]
-    for f, ref in enumerate((xw_s, cw_s)):
+
+    def assemble(f, ref):
         for copy in arrive[3 * f:3 * f + 3]:
             copy.wait()
         ref[...] = (mine[f] + dot(put_ref[...], recv_in[f])).astype(BF16)
+
+    assemble(0, xw_s)
 
     loads["wq"].wait()
     loads["wp"].wait()
@@ -215,13 +223,16 @@
     inv_s[...] = jnp.broadcast_to(inverse, inv_s.shape)
     normed = unit.astype(BF16)
     packed = dot(normed, wq_ref[...]).astype(BF16)
-    cot = cw_s[...]
-    gm_s[...] = dot_nt(cot, wp_ref[...]).astype(BF16)
     for w in range(2):
         at = slice(WIN * w, WIN * w + WIN)
         qkv_s[w] = packed[at]
         qkvt_s[w] = packed[at].T
         normt_s[w] = normed[at].T
+    assemble(1, cw_s)
+    cot = cw_s[...]
+    gm_s[...] = dot_nt(cot, wp_ref[...]).astype(BF16)
+    for w in range(2):
+        at = slice(WIN * w, WIN * w + WIN)
         gmt_s[w] = dot_nt(wp_ref[...], cot[at]).astype(BF16)
 
     lane = lax.broadcasted_iota(jnp.int32, (WIN, 128), 1)
@@ -271,7 +282,7 @@
             gp_s[rows, pl.ds(off + 768, 128)] = grad_value[w].astype(BF16)
         return carry
 
-    lax.fori_loop(0, 3, group, 0)
+    lax.fori_loop(0, 3, group, 0, unroll=True)
 
     for w in range(2):
         gp_s[WIN * w:WIN * w + WIN, 0:384] = gqt_s[w].T
@@ -296,7 +307,6 @@
 
     for w in range(2):
         branch_s[WIN * w:WIN * w + WIN, :] = dot(mixt_s[w].T, wp_ref[...]).astype(BF16)
-    halo_out(0, branch_s)
 
     over_lat = []
     for n in range(nlat - 1):
@@ -304,6 +314,7 @@
         lat_send[n] = (g_s[lev, lat_rows[n], :] + gcore[lat_rows[n], :].astype(F32)).astype(BF16)
         over_lat.append(push(lat_send.at[n], lat_recv.at[n], lat_ss.at[n], lat_rs.at[n], lat_peers[n]))
     core[nlat - 1].wait()
+    halo_out(0, branch_s)
 
     gn = dot_nt(gp_s[...], wq_ref[...])
     unit = unit_s[...]
@@ -329,7 +340,7 @@
         acc_s[...] += dot_nt(jnp.concatenate(lefts, 1), jnp.concatenate(rights, 1))
         return carry
 
-    lax.fori_loop(0, 21, pairs, 0)
+    lax.fori_loop(0, 21, pairs, 0, unroll=3)
     tpart[...] = jnp.zeros_like(tpart)
     for o in range(13):
         tpart[24 * o:24 * o + 12, :] = acc_s[16 * o:16 * o + 12, 0:128]
@@ -426,6 +437,8 @@
         scratch_shapes=[vmem(a.shape, a.dtype) for a in loaded] + [
             vmem((288, 384), BF16),
             vmem((288, 384), BF16),
+            vmem((8, 3328), jnp.int32),
+            vmem((16, POS), F32),
             vmem((168, 128), jnp.int32),
             vmem((12, 24, 128), F32),
             vmem((12, 144, 144), F32),
@@ -476,21 +489,28 @@
 
 
 def publish_kernel(*refs):
-    sems = refs[-1]
-    copies = [pltpu.make_async_copy(refs[n], refs[5 + n], sems.at[n]) for n in range(5)]
-    for copy in copies:
+    results, outs, held = refs[0:5], refs[5:10], refs[10:15]
+    in_sem, out_sem = refs[15:]
+    loads = [pltpu.make_async_copy(results[n], held[n], in_sem.at[n]) for n in range(5)]
+    stores = [pltpu.make_async_copy(held[n], outs[n], out_sem.at[n]) for n in range(5)]
+    for copy in loads:
         copy.start()
-    for copy in copies:
+    for n in range(5):
+        loads[n].wait()
+        stores[n].start()
+    for copy in stores:
         copy.wait()
 
 
 def publish(*results):
+    sem = pltpu.SemaphoreType.DMA
     return pl.pallas_call(
         publish_kernel,
         in_specs=[pl.BlockSpec(memory_space=pl.ANY)] * 5,
         out_specs=[pl.BlockSpec(memory_space=pl.ANY)] * 5,
         out_shape=[jax.ShapeDtypeStruct(r.shape, r.dtype) for r in results],
-        scratch_shapes=[pltpu.SemaphoreType.DMA((5,))],
+        scratch_shapes=[pltpu.VMEM(r.shape, r.dtype) for r in results] + [sem((5,)), sem((5,))],
+        compiler_params=pltpu.CompilerParams(vmem_limit_bytes=56 * 1024 * 1024),
         name="publish",
     )(*results)
 

time: 87.8 us -> 64.8 us (0.74)
  the two profiles are of different devices: /device:TPU:4 before, /device:TPU:6 now
where the time goes in v3:
time: 64.8 us; the launch traced here: 63.8 us
  Pallas kernels  63.2 us (98%)
    pallas_call x1, Pallas kernels, block(): pl.pallas_call(functools.partial(block_kernel, nlat, nlon, norm), in_spec...  61.3 us
    pallas_call x1, Pallas kernels, publish(): pl.pallas_call(publish_kernel, in_specs=[pl.BlockSpec(memory_space=pl.ANY...  1.9 us

profile of v3, /device:TPU:6, one launch (start us, length us, event | category | flops | bytes accessed | tf_op | source)
XLA Modules:
  0.0 63.8 jit_solution(6408252486843567630)
XLA Ops:
  0.6 61.3 %block.1 = (bf16[288,384]{1,0:T(8,128)(2,1)}, bf16[288,384]{1,0:T(8,128)(2,1)}, f32[18,48]{1,0:T(8,128)}, f32[6,48]{1,0:T(8,128)}, f32[12,1,3312]{2,1,0:T(1,128)}) custom-call(bf16[288,384]{1,0:T(8,128)(2,1)} %bitcast.9, bf16[288,384]{1,0:T(8,128)(2,1)} %bitcast.10, bf16[384,1152]{1,0:T(8,128)(2,1)} %wq_hbm.1, bf16[384,384]{1,0:T(8,128)(2,1)} %wp_hbm.1, ...), custom_call_target="tpu_custom_call" | custom-call | tf_op jit(solution)/shard_map/block/pallas_call | solution.py:427
  61.9 1.9 %publish.1 = (bf16[288,384]{1,0:T(8,128)(2,1)}, bf16[288,384]{1,0:T(8,128)(2,1)}, f32[18,48]{1,0:T(8,128)}, f32[6,48]{1,0:T(8,128)}, f32[12,1,3312]{2,1,0:T(1,128)}) custom-call(bf16[288,384]{1,0:T(8,128)(2,1)} %get-tuple-element.15.refs_0_, bf16[288,384]{1,0:T(8,128)(2,1)} %get-tuple-element.16.refs_1_, f32[18,48]{1,0:T(8,128)} %get-tuple-element.17.refs_2_, ...), custom_call_target="tpu_custom_call" | custom-call | tf_op jit(solution)/shard_map/publish/pallas_call | solution.py:507

commit v4 on v3

--- a/solution.py
+++ b/solution.py
@@ -87,18 +87,9 @@
                  xw_s, cw_s, words_s, rows_of_table, idx_s, tail_s, bias_s, qkv_s, qkvt_s, gm_s, gmt_s, mixt_s, gqt_s, gp_s,
                  unit_s, inv_s, normt_s, gs_s, acc_s, branch_s, rows_s, g_s, tpart,
                  send_in, recv_in, send, recv, gsend, gcore, lat_send, lat_recv, turn, turned, ypart, ysend, yrecv,
-                 zpart, zrecv, trecv, tsum, tzrecv, tfull,
+                 zpart, zrecv, gs_send, gs_recv, tsend, trecv, tz, tfull,
                  load_sem, in_ss, in_rs, halo_ss, halo_rs, core_ss, core_rs, lat_ss, lat_rs,
-                 y_ss, y_rs, z_ss, z_rs, t_ss, t_rs, tz_ss, tz_rs, tg_ss, tg_rs):
-    names = ("x", "c", "take", "own", "put", "tab", "idx", "reg", "wq", "wp", "own_t", "take_t", "put_t")
-    from_to = ((x_hbm, x_ref), (c_hbm, c_ref), (take_hbm, take_ref), (own_hbm, own_ref), (put_hbm, put_ref),
-                (tab_hbm, tab_ref), (idx_hbm, idx_ref), (reg_hbm, reg_ref), (wq_hbm, wq_ref), (wp_hbm, wp_ref),
-                (own_t_hbm, own_t_ref), (take_t_hbm, take_t_ref), (put_t_hbm, put_t_ref))
-    loads = {}
-    for n, (name, (src, dst)) in enumerate(zip(names, from_to)):
-        loads[name] = pltpu.make_async_copy(src, dst, load_sem.at[n])
-        loads[name].start()
-
+                 y_ss, y_rs, z_ss, z_rs, t_ss, t_rs, tz_ss, tz_rs, tg_ss, tg_rs, gs_ss, gs_rs):
     nz = nlon // 8
     lev, lat, lon = lax.axis_index("lev"), lax.axis_index("lat"), lax.axis_index("lon")
     z, y = lon // 8, lax.rem(lon, 8)
@@ -120,6 +111,15 @@
     greet = after[1:] + before[1:] + lat_peers + owners + z_peers
     for device in greet:
         pl.semaphore_signal(barrier, inc=1, device_id=device, device_id_type=MESH)
+
+    names = ("x", "c", "take", "own", "put", "tab", "idx", "reg", "wq", "wp", "own_t", "take_t", "put_t")
+    from_to = ((x_hbm, x_ref), (c_hbm, c_ref), (take_hbm, take_ref), (own_hbm, own_ref), (put_hbm, put_ref),
+                (tab_hbm, tab_ref), (idx_hbm, idx_ref), (reg_hbm, reg_ref), (wq_hbm, wq_ref), (wp_hbm, wp_ref),
+                (own_t_hbm, own_t_ref), (take_t_hbm, take_t_ref), (put_t_hbm, put_t_ref))
+    loads = {}
+    for n, (name, (src, dst)) in enumerate(zip(names, from_to)):
+        loads[name] = pltpu.make_async_copy(src, dst, load_sem.at[n])
+        loads[name].start()
 
     def push(src, dst, ss, rs, device):
         copy = pltpu.make_async_remote_copy(
@@ -238,8 +238,8 @@
     lane = lax.broadcasted_iota(jnp.int32, (WIN, 128), 1)
     line_of = lax.broadcasted_iota(jnp.int32, (128, WIN), 0)
 
-    def group(g, carry):
-        off = pl.multiple_of(g * 128, 128)
+    for g in range(3):
+        off = 128 * g
         grad_key = [None, None]
         grad_value = [None, None]
         for a in range(4):
@@ -254,7 +254,7 @@
                 v = qkv_s[w, :, pl.ds(off + 768, 128)]
                 qt = qkvt_s[w, pl.ds(off, 128), :]
                 gmt = gmt_s[w, pl.ds(off, 128), :]
-                here = pl.multiple_of(off + 32 * a, 32)
+                here = off + 32 * a
                 kt = qkvt_s[w, pl.ds(384 + here, 32), :]
                 vt = qkvt_s[w, pl.ds(768 + here, 32), :]
                 gm = gm_s[pl.ds(WIN * w, WIN), pl.ds(off, 128)]
@@ -274,15 +274,16 @@
                 grad_key[w] = gk if a == 0 else jnp.where(own_lane, gk, grad_key[w])
                 grad_value[w] = gv if a == 0 else jnp.where(own_lane, gv, grad_value[w])
                 total = gs if w == 0 else total + gs
-            gs_s[0:WIN, pl.ds(h, 1), :] = total[:, 0:128].reshape(WIN, 1, 128)
-            gs_s[WIN:168, pl.ds(h, 1), :] = pack_tail(total[:, 128:144]).reshape(24, 1, 128)
+            at = slice(h % 6, h % 6 + 1)
+            gs_s[h // 6, 0:WIN, at, :] = total[:, 0:128].reshape(WIN, 1, 128)
+            gs_s[h // 6, WIN:168, at, :] = pack_tail(total[:, 128:144]).reshape(24, 1, 128)
         for w in range(2):
             rows = slice(WIN * w, WIN * w + WIN)
             gp_s[rows, pl.ds(off + 384, 128)] = grad_key[w].astype(BF16)
             gp_s[rows, pl.ds(off + 768, 128)] = grad_value[w].astype(BF16)
-        return carry
-
-    lax.fori_loop(0, 3, group, 0, unroll=True)
+
+    gs_send[...] = gs_s[1 - lev].reshape(1344, 128).astype(BF16)
+    swap = push(gs_send, gs_recv, gs_ss.at[0], gs_rs.at[0], core_peer)
 
     for w in range(2):
         gp_s[WIN * w:WIN * w + WIN, 0:384] = gqt_s[w].T
@@ -330,24 +331,35 @@
         entry = idx_s[pl.ds(pl.multiple_of(r * 8, 8), 8), :]
         low = jnp.bitwise_and(entry, 255)
         high = jnp.right_shift(entry, 8)
+        other = gs_recv[pl.ds(pl.multiple_of(r * 64, 64), 64), :].astype(F32)
+        both = gs_s[lev, pl.ds(r * 8, 8)] + other.reshape(8, 8, 128)
         lefts = []
         rights = []
         for s in range(8):
-            value = gs_s[r * 8 + s]
+            value = both[s]
             lefts.append(jnp.concatenate(
-                [jnp.where(high[s:s + 1, :] == k, value, 0.0).astype(BF16) for k in range(13)], 0))
+                [jnp.where(high[s:s + 1, :] == k, value, 0.0) for k in range(13)], 0).astype(BF16))
             rights.append(jnp.where(low[s:s + 1, :] == low_of, 1.0, 0.0).astype(BF16))
         acc_s[...] += dot_nt(jnp.concatenate(lefts, 1), jnp.concatenate(rights, 1))
         return carry
 
+    swap.wait()
     lax.fori_loop(0, 21, pairs, 0, unroll=3)
     tpart[...] = jnp.zeros_like(tpart)
-    for o in range(13):
-        tpart[24 * o:24 * o + 12, :] = acc_s[16 * o:16 * o + 12, 0:128]
-        tpart[24 * o + 12:24 * o + 24, :] = acc_s[16 * o:16 * o + 12, 128:256]
-    table = [push(tpart.at[pl.ds(pl.multiple_of(24 * step(owner, d, 16), 24), 24)],
-                  trecv.at[d - 1], t_ss.at[d - 1], t_rs.at[d - 1], owners[d - 1])
-             for d in range(1, 16)]
+    for k in range(13):
+        tpart[16 * k:16 * k + 8, :] = acc_s[8 * k:8 * k + 8, 0:128]
+        tpart[16 * k + 8:16 * k + 16, :] = acc_s[8 * k:8 * k + 8, 128:256]
+    tsend[...] = tpart[...].astype(BF16)
+    table = [push(tsend.at[pl.ds(pl.multiple_of(32 * step(y, d, 8), 32), 32)],
+                  trecv.at[d - 1], t_ss.at[d - 1], t_rs.at[d - 1], y_peers[d - 1])
+             for d in range(1, 8)]
+
+    part = tpart[pl.ds(pl.multiple_of(32 * y, 32), 32), :]
+    for n in range(7):
+        table[n].wait()
+        part = part + trecv[n].astype(F32)
+    tz[z] = part
+    over_z = [push(tz.at[z], tz.at[z], tz_ss.at[n], tz_rs.at[n], z_peers[n]) for n in range(nz - 1)]
 
     total = g_s[lev, lat_rows[-1], :] + gcore[lat_rows[-1], :].astype(F32)
     for n in range(nlat - 1):
@@ -369,13 +381,15 @@
     over_y = [push(ysend.at[step(y, d, 8)], yrecv.at[d - 1], y_ss.at[d - 1], y_rs.at[d - 1], y_peers[d - 1])
               for d in range(1, 8)]
 
-    own_block = pl.ds(pl.multiple_of(24 * owner, 24), 24)
-    part = tpart[own_block, :]
-    for n in range(15):
-        table[n].wait()
-        part = part + trecv[n]
-    tsum[0] = part
-    over_z = [push(tsum.at[0], tzrecv.at[n], tz_ss.at[n], tz_rs.at[n], z_peers[n]) for n in range(nz - 1)]
+    for copy in over_z:
+        copy.wait()
+    part = tz[0]
+    for n in range(1, nz):
+        part = part + tz[n]
+    own_block = pl.ds(pl.multiple_of(32 * owner, 32), 32)
+    tfull[own_block, :] = part.astype(BF16)
+    gathered = [push(tfull.at[own_block], tfull.at[own_block], tg_ss.at[n], tg_rs.at[n], owners[n])
+                for n in range(15)]
 
     total = ypart[y]
     for n in range(7):
@@ -386,13 +400,6 @@
                  zrecv.at[d - 1], z_ss.at[d - 1], z_rs.at[d - 1], z_peers[d - 1])
             for d in range(1, nz)]
 
-    for n in range(nz - 1):
-        over_z[n].wait()
-        part = part + tzrecv[n]
-    tsum[1] = part
-    gathered = [push(tsum.at[1], tfull.at[own_block], tg_ss.at[n], tg_rs.at[n], owners[n])
-                for n in range(15)]
-
     loads["own_t"].wait()
     loads["take_t"].wait()
     for f, (base, ref, out) in enumerate(((x_ref, branch_s, xo_ref), (c_ref, rows_s, co_ref))):
@@ -409,14 +416,14 @@
     gq_ref[...] = total[0:18]
     gp_ref[...] = total[18:24]
 
-    tfull[own_block, :] = part
     for n in range(15):
         gathered[n].wait()
-    for o in range(13):
-        width = min(128, POS - 256 * o - 128)
+    full = tfull[...].astype(F32)
+    for k in range(26):
+        width = min(128, POS - 128 * k)
         for h in range(HEADS):
-            to_ref[h, :, 256 * o:256 * o + 128] = tfull[24 * o + h:24 * o + h + 1, :]
-            to_ref[h, :, 256 * o + 128:256 * o + 128 + width] = tfull[24 * o + 12 + h:24 * o + 13 + h, 0:width]
+            at = 256 * (h // 6) + 8 * k + h % 6
+            to_ref[h, :, 128 * k:128 * k + width] = full[at:at + 1, 0:width]
 
 
 def block(nlat, nlon, norm, *operands):
@@ -452,12 +459,12 @@
             vmem((288, 384), F32),
             vmem((288, 128), F32),
             vmem((2, 384, 144), BF16),
-            vmem((168, 16, 128), F32),
-            vmem((208, 256), F32),
+            vmem((2, 168, 8, 128), F32),
+            vmem((104, 256), F32),
             vmem((288, 384), BF16),
             vmem((288, 384), BF16),
             vmem((2, 384, 768), F32),
-            vmem((384, 128), F32),
+            vmem((256, 128), F32),
             vmem((2, 208, 384), BF16),
             vmem((2, 208, 384), BF16),
             vmem((2, 208, 384), BF16),
@@ -473,14 +480,16 @@
             vmem((7, 48, 128), BF16),
             vmem((48, 128), F32),
             vmem((nz - 1, 24, 128), F32),
-            vmem((15, 24, 128), F32),
-            vmem((2, 24, 128), F32),
-            vmem((nz - 1, 24, 128), F32),
-            vmem((384, 128), F32),
+            vmem((1344, 128), BF16),
+            vmem((1344, 128), BF16),
+            vmem((256, 128), BF16),
+            vmem((7, 32, 128), BF16),
+            vmem((nz, 32, 128), F32),
+            vmem((512, 128), BF16),
             sem((13,)), sem((6,)), sem((6,)), sem((6,)), sem((6,)), sem((nlat,)), sem((nlat,)),
             sem((nlat - 1,)), sem((nlat - 1,)),
             sem((7,)), sem((7,)), sem((nz - 1,)), sem((nz - 1,)),
-            sem((15,)), sem((15,)), sem((nz - 1,)), sem((nz - 1,)), sem((15,)), sem((15,)),
+            sem((7,)), sem((7,)), sem((nz - 1,)), sem((nz - 1,)), sem((15,)), sem((15,)), sem((1,)), sem((1,)),
         ],
         compiler_params=pltpu.CompilerParams(
             collective_id=0, has_side_effects=True, vmem_limit_bytes=56 * 1024 * 1024),

time: 64.8 us -> 63.3 us (0.977); the launches traced: 63.8 us -> 63.2 us
  Pallas kernels: 63.2 us -> 62.5 us
    pallas_call x1, Pallas kernels: 61.3 us -> 60.6 us  [block(): pl.pallas_call(functools.partial(block_kernel, nlat, nlon, norm), in_spec...]
where the time goes in v4:
time: 63.3 us; the launch traced here: 63.2 us
  Pallas kernels  62.5 us (99%)
  between operations  0.64 us (1%)
    pallas_call x1, Pallas kernels, block(): pl.pallas_call(functools.partial(block_kernel, nlat, nlon, norm), in_spec...  60.6 us
    pallas_call x1, Pallas kernels, publish(): pl.pallas_call(publish_kernel, in_specs=[pl.BlockSpec(memory_space=pl.ANY...  1.9 us

profile of v4, /device:TPU:6, one launch (start us, length us, event | category | flops | bytes accessed | tf_op | source)
XLA Modules:
  0.0 63.2 jit_solution(3595956997360566759)
XLA Ops:
  0.6 60.6 %block.1 = (bf16[288,384]{1,0:T(8,128)(2,1)}, bf16[288,384]{1,0:T(8,128)(2,1)}, f32[18,48]{1,0:T(8,128)}, f32[6,48]{1,0:T(8,128)}, f32[12,1,3312]{2,1,0:T(1,128)}) custom-call(bf16[288,384]{1,0:T(8,128)(2,1)} %bitcast.9, bf16[288,384]{1,0:T(8,128)(2,1)} %bitcast.10, bf16[384,1152]{1,0:T(8,128)(2,1)} %wq_hbm.1, bf16[384,384]{1,0:T(8,128)(2,1)} %wp_hbm.1, ...), custom_call_target="tpu_custom_call" | custom-call | tf_op jit(solution)/shard_map/block/pallas_call | solution.py:434
  61.3 1.9 %publish.1 = (bf16[288,384]{1,0:T(8,128)(2,1)}, bf16[288,384]{1,0:T(8,128)(2,1)}, f32[18,48]{1,0:T(8,128)}, f32[6,48]{1,0:T(8,128)}, f32[12,1,3312]{2,1,0:T(1,128)}) custom-call(bf16[288,384]{1,0:T(8,128)(2,1)} %get-tuple-element.15.refs_0_, bf16[288,384]{1,0:T(8,128)(2,1)} %get-tuple-element.16.refs_1_, f32[18,48]{1,0:T(8,128)} %get-tuple-element.17.refs_2_, ...), custom_call_target="tpu_custom_call" | custom-call | tf_op jit(solution)/shard_map/publish/pallas_call | solution.py:516

commit v5 on v4

--- a/solution.py
+++ b/solution.py
@@ -298,16 +298,9 @@
             for n, rows in enumerate(lat_rows)]
 
     loads["put_t"].wait()
-    halo = []
-
-    def halo_out(f, ref):
-        send[f] = dot(put_t_ref[...], ref[...]).astype(BF16)
-        for n, (at, size) in enumerate(PIECES):
-            halo.append(push(send.at[f, pl.ds(at, size)], recv.at[f, pl.ds(at, size)],
-                             halo_ss.at[3 * f + n], halo_rs.at[3 * f + n], after[n]))
-
     for w in range(2):
         branch_s[WIN * w:WIN * w + WIN, :] = dot(mixt_s[w].T, wp_ref[...]).astype(BF16)
+    send[0] = dot(put_t_ref[...], branch_s[...]).astype(BF16)
 
     over_lat = []
     for n in range(nlat - 1):
@@ -315,14 +308,6 @@
         lat_send[n] = (g_s[lev, lat_rows[n], :] + gcore[lat_rows[n], :].astype(F32)).astype(BF16)
         over_lat.append(push(lat_send.at[n], lat_recv.at[n], lat_ss.at[n], lat_rs.at[n], lat_peers[n]))
     core[nlat - 1].wait()
-    halo_out(0, branch_s)
-
-    gn = dot_nt(gp_s[...], wq_ref[...])
-    unit = unit_s[...]
-    rows_s[...] = (inv_s[:, 0:1] * (
-        gn - jnp.mean(gn, axis=-1, keepdims=True)
-        - unit * jnp.mean(gn * unit, axis=-1, keepdims=True))).astype(BF16)
-    halo_out(1, rows_s)
 
     acc_s[...] = jnp.zeros_like(acc_s)
     low_of = lax.broadcasted_iota(jnp.int32, (256, 128), 0)
@@ -344,7 +329,7 @@
         return carry
 
     swap.wait()
-    lax.fori_loop(0, 21, pairs, 0, unroll=3)
+    lax.fori_loop(0, 21, pairs, 0, unroll=7)
     tpart[...] = jnp.zeros_like(tpart)
     for k in range(13):
         tpart[16 * k:16 * k + 8, :] = acc_s[8 * k:8 * k + 8, 0:128]
@@ -353,6 +338,21 @@
     table = [push(tsend.at[pl.ds(pl.multiple_of(32 * step(y, d, 8), 32), 32)],
                   trecv.at[d - 1], t_ss.at[d - 1], t_rs.at[d - 1], y_peers[d - 1])
              for d in range(1, 8)]
+
+    def halo_out(f):
+        return [push(send.at[f, pl.ds(at, size)], recv.at[f, pl.ds(at, size)],
+                     halo_ss.at[3 * f + n], halo_rs.at[3 * f + n], after[n])
+                for n, (at, size) in enumerate(PIECES)]
+
+    halo = halo_out(0)
+    gn = dot_nt(gp_s[...], wq_ref[...])
+    unit = unit_s[...]
+    rows_s[...] = (inv_s[:, 0:1] * (
+        gn - jnp.mean(gn, axis=-1, keepdims=True)
+        - unit * jnp.mean(gn * unit, axis=-1, keepdims=True))).astype(BF16)
+    send[1] = dot(put_t_ref[...], rows_s[...]).astype(BF16)
+
+    halo += halo_out(1)
 
     part = tpart[pl.ds(pl.multiple_of(32 * y, 32), 32), :]
     for n in range(7):

time: 63.3 us -> 64.3 us (1.016)
  Pallas kernels: 62.5 us -> 63.5 us
    pallas_call x1, Pallas kernels: 60.6 us -> 61.6 us  [block(): pl.pallas_call(functools.partial(block_kernel, nlat, nlon, norm), in_spec...]
where the time goes in v5:
time: 64.3 us; the launch traced here: 64.2 us
  Pallas kernels  63.5 us (99%)
    pallas_call x1, Pallas kernels, block(): pl.pallas_call(functools.partial(block_kernel, nlat, nlon, norm), in_spec...  61.6 us
    pallas_call x1, Pallas kernels, publish(): pl.pallas_call(publish_kernel, in_specs=[pl.BlockSpec(memory_space=pl.ANY...  1.9 us

profile of v5, /device:TPU:6, one launch (start us, length us, event | category | flops | bytes accessed | tf_op | source)
XLA Modules:
  0.0 64.2 jit_solution(8591779771736951603)
XLA Ops:
  0.6 61.6 %block.1 = (bf16[288,384]{1,0:T(8,128)(2,1)}, bf16[288,384]{1,0:T(8,128)(2,1)}, f32[18,48]{1,0:T(8,128)}, f32[6,48]{1,0:T(8,128)}, f32[12,1,3312]{2,1,0:T(1,128)}) custom-call(bf16[288,384]{1,0:T(8,128)(2,1)} %bitcast.9, bf16[288,384]{1,0:T(8,128)(2,1)} %bitcast.10, bf16[384,1152]{1,0:T(8,128)(2,1)} %wq_hbm.1, bf16[384,384]{1,0:T(8,128)(2,1)} %wp_hbm.1, ...), custom_call_target="tpu_custom_call" | custom-call | tf_op jit(solution)/shard_map/block/pallas_call | solution.py:434
  62.3 1.9 %publish.1 = (bf16[288,384]{1,0:T(8,128)(2,1)}, bf16[288,384]{1,0:T(8,128)(2,1)}, f32[18,48]{1,0:T(8,128)}, f32[6,48]{1,0:T(8,128)}, f32[12,1,3312]{2,1,0:T(1,128)}) custom-call(bf16[288,384]{1,0:T(8,128)(2,1)} %get-tuple-element.15.refs_0_, bf16[288,384]{1,0:T(8,128)(2,1)} %get-tuple-element.16.refs_1_, f32[18,48]{1,0:T(8,128)} %get-tuple-element.17.refs_2_, ...), custom_call_target="tpu_custom_call" | custom-call | tf_op jit(solution)/shard_map/publish/pallas_call | solution.py:516

commit v6 on v5

--- a/solution.py
+++ b/solution.py
@@ -309,6 +309,13 @@
         over_lat.append(push(lat_send.at[n], lat_recv.at[n], lat_ss.at[n], lat_rs.at[n], lat_peers[n]))
     core[nlat - 1].wait()
 
+    def halo_out(f):
+        return [push(send.at[f, pl.ds(at, size)], recv.at[f, pl.ds(at, size)],
+                     halo_ss.at[3 * f + n], halo_rs.at[3 * f + n], after[n])
+                for n, (at, size) in enumerate(PIECES)]
+
+    halo = halo_out(0)
+
     acc_s[...] = jnp.zeros_like(acc_s)
     low_of = lax.broadcasted_iota(jnp.int32, (256, 128), 0)
 
@@ -329,7 +336,7 @@
         return carry
 
     swap.wait()
-    lax.fori_loop(0, 21, pairs, 0, unroll=7)
+    lax.fori_loop(0, 21, pairs, 0, unroll=3)
     tpart[...] = jnp.zeros_like(tpart)
     for k in range(13):
         tpart[16 * k:16 * k + 8, :] = acc_s[8 * k:8 * k + 8, 0:128]
@@ -339,12 +346,6 @@
                   trecv.at[d - 1], t_ss.at[d - 1], t_rs.at[d - 1], y_peers[d - 1])
              for d in range(1, 8)]
 
-    def halo_out(f):
-        return [push(send.at[f, pl.ds(at, size)], recv.at[f, pl.ds(at, size)],
-                     halo_ss.at[3 * f + n], halo_rs.at[3 * f + n], after[n])
-                for n, (at, size) in enumerate(PIECES)]
-
-    halo = halo_out(0)
     gn = dot_nt(gp_s[...], wq_ref[...])
     unit = unit_s[...]
     rows_s[...] = (inv_s[:, 0:1] * (

time: 64.3 us -> 63.5 us (0.988)
  Pallas kernels: 63.5 us -> 62.7 us
    pallas_call x1, Pallas kernels: 61.6 us -> 60.8 us  [block(): pl.pallas_call(functools.partial(block_kernel, nlat, nlon, norm), in_spec...]
where the time goes in v6:
time: 63.5 us; the launch traced here: 63.3 us
  Pallas kernels  62.7 us (99%)
  between operations  0.64 us (1%)
    pallas_call x1, Pallas kernels, block(): pl.pallas_call(functools.partial(block_kernel, nlat, nlon, norm), in_spec...  60.8 us
    pallas_call x1, Pallas kernels, publish(): pl.pallas_call(publish_kernel, in_specs=[pl.BlockSpec(memory_space=pl.ANY...  1.9 us

profile of v6, /device:TPU:6, one launch (start us, length us, event | category | flops | bytes accessed | tf_op | source)
XLA Modules:
  0.0 63.3 jit_solution(17407985727784769183)
XLA Ops:
  0.6 60.8 %block.1 = (bf16[288,384]{1,0:T(8,128)(2,1)}, bf16[288,384]{1,0:T(8,128)(2,1)}, f32[18,48]{1,0:T(8,128)}, f32[6,48]{1,0:T(8,128)}, f32[12,1,3312]{2,1,0:T(1,128)}) custom-call(bf16[288,384]{1,0:T(8,128)(2,1)} %bitcast.9, bf16[288,384]{1,0:T(8,128)(2,1)} %bitcast.10, bf16[384,1152]{1,0:T(8,128)(2,1)} %wq_hbm.1, bf16[384,384]{1,0:T(8,128)(2,1)} %wp_hbm.1, ...), custom_call_target="tpu_custom_call" | custom-call | tf_op jit(solution)/shard_map/block/pallas_call | solution.py:435
  61.4 1.9 %publish.1 = (bf16[288,384]{1,0:T(8,128)(2,1)}, bf16[288,384]{1,0:T(8,128)(2,1)}, f32[18,48]{1,0:T(8,128)}, f32[6,48]{1,0:T(8,128)}, f32[12,1,3312]{2,1,0:T(1,128)}) custom-call(bf16[288,384]{1,0:T(8,128)(2,1)} %get-tuple-element.15.refs_0_, bf16[288,384]{1,0:T(8,128)(2,1)} %get-tuple-element.16.refs_1_, f32[18,48]{1,0:T(8,128)} %get-tuple-element.17.refs_2_, ...), custom_call_target="tpu_custom_call" | custom-call | tf_op jit(solution)/shard_map/publish/pallas_call | solution.py:517
